TPU v7x, 32 devices: a whole 2x2x4 slice. The times are simulated.
32 devices in a mesh: dp: 8 (over z, x), tensor: 4 (over y, core).
Axes of the slice: x: 2, y: 2, z: 4, core: 2. Of those that a mesh axis runs over, the one named last changes fastest.
Arguments:
- tokens: bfloat16 [32768, 768], P(('dp', 'tensor')), may hold values from -6 to 6
- lengths: int32 [64], P(('dp', 'tensor')), may hold values from 16 to 512, as said below
- frozen_attention_weights: bfloat16 [2, 3072, 768], P(None, ('dp', 'tensor')), may hold values from -6 to 6
- adapter_down_weights: bfloat16 [2, 2, 768, 8], replicated, may hold values from -0.21875 to 0.21875
- adapter_up_weights: bfloat16 [2, 2, 8, 768], replicated, may hold values from -1 to 1
- frozen_expand_weight: bfloat16 [2, 768, 3072], P(None, None, 'tensor'), may hold values from -0.21875 to 0.21875
- frozen_project_weight: bfloat16 [2, 3072, 768], P(None, 'tensor'), may hold values from -0.109375 to 0.109375
- frozen_norm_gains: float32 [2, 2, 768], replicated, may hold values from 0.5 to 1.5
- cotangent: bfloat16 [32768, 768], P(('dp', 'tensor')), may hold values from -6 to 6
Outputs:
- hidden_out: bfloat16 [32768, 768], P(('dp', 'tensor'))
- input_grad: float32 [32768, 768], P(('dp', 'tensor'))
- lora_a_grad: float32 [2, 2, 768, 8], replicated
- lora_b_grad: float32 [2, 2, 8, 768], replicated
Inputs may be any that keep to these rules, and one draw needn't show every extreme that they name: The first lengths[r] tokens of row r are valid, the rest are padding for keys.
All inputs are finite; a program needn't handle non-finite values.
Results may differ from a plain program's by a relative error of at most 0.033.
Values may be sent and summed in bfloat16 or wider, within the bound.
A program may use at most 256 MiB of HBM per device.

v0:
```python
import functools
import jax
import jax.numpy as jnp
from jax import lax
from jax.experimental import pallas as pl
from jax.experimental.pallas import tpu as pltpu
from jax.sharding import PartitionSpec as P

WIDTH = 768
HEADS = 12
HEAD_DIM = 64
SEQ = 512
RANK = 8
EPS = 1e-05
CHUNK = 768
BF = jnp.bfloat16
F32 = jnp.float32
VMEM_LIMIT = 60 * 1024 * 1024
EXP2_SCALE = 1.4426950408889634 * HEAD_DIM ** (-0.5)


def dot(a, b):
    return jnp.dot(a, b, preferred_element_type=F32)


def dot_nt(a, b):
    return lax.dot_general(a, b, (((1,), (1,)), ((), ())), preferred_element_type=F32)


def dot_tn(a, b):
    return lax.dot_general(a, b, (((0,), (0,)), ((), ())), preferred_element_type=F32)


def mean_rows(v):
    return jnp.sum(v, axis=-1, keepdims=True) * (1.0 / WIDTH)


def params(n, collective=None):
    more = {} if collective is None else {"collective_id": collective, "has_side_effects": True}
    return pltpu.CompilerParams(
        dimension_semantics=("arbitrary",) * n, vmem_limit_bytes=VMEM_LIMIT, **more
    )


MESH = pl.DeviceIdType.MESH
Z_SIZE = 4


class Place:
    def __init__(self, axes):
        dp, t = lax.axis_index(axes[0]), lax.axis_index(axes[1])
        self.dp, self.t = dp, t
        self.z, self.x = dp // 2, dp % 2
        self.y, self.core = t // 2, t % 2
        self.to_core = (dp, t + 1 - 2 * self.core)
        self.to_y = (dp, t + 2 - 4 * self.y)
        self.to_x = (dp + 1 - 2 * self.x, t)
        self.to_zpair = (dp + 2 - 4 * (self.z % 2), t)
        self.to_up = (dp + 2, t)
        self.to_down = (dp - 2, t)


def greet(place, line):
    barrier = pltpu.get_barrier_semaphore()
    for device in (place.to_core, place.to_y, place.to_x):
        pl.semaphore_signal(barrier, inc=1, device_id=device, device_id_type=MESH)
    if line:
        @pl.when(place.z < Z_SIZE - 1)
        def _():
            pl.semaphore_signal(barrier, inc=1, device_id=place.to_up, device_id_type=MESH)

        @pl.when(place.z > 0)
        def _():
            pl.semaphore_signal(barrier, inc=1, device_id=place.to_down, device_id_type=MESH)

        inner = (place.z > 0) & (place.z < Z_SIZE - 1)

        @pl.when(inner)
        def _():
            pl.semaphore_wait(barrier, 5)

        @pl.when(jnp.logical_not(inner))
        def _():
            pl.semaphore_wait(barrier, 4)
    else:
        pl.semaphore_signal(barrier, inc=1, device_id=place.to_zpair, device_id_type=MESH)
        pl.semaphore_wait(barrier, 4)


def remote(src, dst, send, recv, device):
    return pltpu.make_async_remote_copy(
        src_ref=src, dst_ref=dst, send_sem=send, recv_sem=recv, device_id=device, device_id_type=MESH
    )


SLICE = 128
FFN_SEMS = [
    pltpu.SemaphoreType.DMA((3, 4)),
    pltpu.SemaphoreType.DMA((12,)),
    pltpu.SemaphoreType.DMA((14,)),
    pltpu.SemaphoreType.DMA((14,)),
]
FFN_TICKS = 8


def ffn_gather(place, layer, w1, w2, out, sems, tick):
    send, recv, core_send, core_recv = sems
    g = place.x * 2 + place.z % 2
    gd = 3 - g
    gx = (1 - place.x) * 2 + place.z % 2
    gz = place.x * 2 + 1 - place.z % 2

    def spot(slot, s):
        return out.at[slot + 1, s // 6, pl.ds(pl.multiple_of((s % 6) * SLICE, SLICE), SLICE)]

    def over_y(i):
        s = 3 * g + i if i < 3 else 3 * gd
        first = place.x == (0 if i < 3 else 1)
        for here, ref in ((first, w1), (jnp.logical_not(first), w2)):
            @pl.when(here)
            def _():
                src = ref.at[layer, pl.ds(pl.multiple_of((s % 6) * SLICE, SLICE), SLICE)]
                remote(src, spot(1, s), send.at[0, i], recv.at[s], place.to_y).start()

    def arrived(s):
        remote(spot(1, s), spot(1, s), send.at[0, 0], recv.at[s], place.to_y).wait_recv()

    def over(way, i, s):
        device = place.to_x if way == 1 else place.to_zpair
        remote(spot(1, s), spot(1, s), send.at[way, i], recv.at[s], device).start()

    def share(s):
        remote(spot(1, s), spot(2, s), core_send.at[s], core_recv.at[s], place.to_core).start()

    if tick == 0:
        for i in range(4):
            over_y(i)
        for m, ref in enumerate((w1, w2)):
            remote(ref.at[layer], out.at[1, m], core_send.at[12 + m], core_recv.at[12 + m], place.to_core).start()
    elif tick < 4:
        s = 3 * g + tick - 1
        arrived(s)
        over(1, tick - 1, s)
        over(2, tick - 1, s)
        share(s)
        if tick == 3:
            for s in (3 * gx, 3 * gz):
                arrived(s)
                share(s)
    elif tick == 4:
        s = 3 * gz + 1
        arrived(s)
        over(1, 3, s)
        share(s)
        for s in (3 * gd, 3 * gx + 1):
            arrived(s)
            share(s)
    elif tick == 5:
        s = 3 * gx + 2
        arrived(s)
        over(2, 3, s)
        share(s)
        s = 3 * gz + 2
        arrived(s)
        share(s)
    elif tick == 6:
        for s in (3 * gd + 1, 3 * gd + 2):
            arrived(s)
            share(s)
    else:
        for s in range(12):
            remote(spot(1, s), spot(2, s), core_send.at[s], core_recv.at[s], place.to_core).wait()
        for m, ref in enumerate((w1, w2)):
            remote(ref.at[layer], out.at[1, m], core_send.at[12 + m], core_recv.at[12 + m], place.to_core).wait()
        for way in range(3):
            for i in range(4):
                remote(spot(1, 0), spot(1, 0), send.at[way, i], recv.at[0], place.to_y).wait_send()


ATT_SEMS = [
    pltpu.SemaphoreType.DMA((2, 4)),
    pltpu.SemaphoreType.DMA((4,)),
    pltpu.SemaphoreType.DMA((2, 4)),
    pltpu.SemaphoreType.DMA((2, 4)),
    pltpu.SemaphoreType.DMA((2, 4)),
    pltpu.SemaphoreType.DMA((2, 4)),
    pltpu.SemaphoreType.DMA((5, 4)),
    pltpu.SemaphoreType.DMA((5, 4)),
    pltpu.SemaphoreType.DMA,
]
ATT_TICKS = 7


def attention_gather(place, layer, block, out, sems, tick):
    z_send, z_recv, n_send, n_recv, h_send, h_recv, c_send, c_recv, own_sem = sems
    rows = block.shape[1]
    half = rows // 2
    z, x, y, core = place.z, place.x, place.y, place.core

    def spot(sz, sx, sy, sc, start=0, size=rows):
        at = ((sz * 2 + sx) * 4 + sy * 2 + sc) * rows + start
        return out.at[pl.ds(pl.multiple_of(at, 16), size)]

    def line(sz):
        return spot(sz, x, y, core)

    def side(way, sz):
        return spot(sz, 1 - x, y, core) if way == 0 else spot(sz, x, 1 - y, core)

    def far(way, sz):
        return spot(sz, 1 - x, 1 - y, core, way * half, half)

    devices = (place.to_x, place.to_y)

    def at_distance(d, action):
        if d == 0:
            action(z)
            return
        @pl.when(z >= d)
        def _():
            action(z - d)

        @pl.when(z + d < Z_SIZE)
        def _():
            action(z + d)

    def line_step(sz, own):
        mine = block.at[layer] if own else line(sz)
        if not own:
            remote(line(sz), line(sz), z_send.at[0, sz], z_recv.at[sz], place.to_core).wait_recv()

        @pl.when((sz <= z) & (z < Z_SIZE - 1))
        def _():
            remote(mine, line(sz), z_send.at[0, sz], z_recv.at[sz], place.to_up).start()

        @pl.when((sz >= z) & (z > 0))
        def _():
            remote(mine, line(sz), z_send.at[1, sz], z_recv.at[sz], place.to_down).start()

        for way in range(2):
            remote(mine, line(sz), n_send.at[way, sz], n_recv.at[way, sz], devices[way]).start()
        remote(mine, line(sz), c_send.at[0, sz], c_recv.at[0, sz], place.to_core).start()

    def side_step(sz):
        for way in range(2):
            remote(side(way, sz), side(way, sz), n_send.at[way, sz], n_recv.at[way, sz], devices[way]).wait_recv()
            at = spot(sz, 1 - x, y, core, 0, half) if way == 0 else spot(sz, x, 1 - y, core, half, half)
            remote(at, at, h_send.at[way, sz], h_recv.at[way, sz], devices[1 - way]).start()
            remote(side(way, sz), side(way, sz), c_send.at[1 + way, sz], c_recv.at[1 + way, sz], place.to_core).start()

    def far_step(sz):
        for way in range(2):
            remote(far(way, sz), far(way, sz), h_send.at[way, sz], h_recv.at[way, sz], place.to_core).wait_recv()
            remote(far(way, sz), far(way, sz), c_send.at[3 + way, sz], c_recv.at[3 + way, sz], place.to_core).start()

    if tick == 0:
        pltpu.make_async_copy(block.at[layer], line(z), own_sem).start()
    if tick < 4:
        at_distance(tick, functools.partial(line_step, own=tick == 0))
    if 1 <= tick < 5:
        at_distance(tick - 1, side_step)
    if 2 <= tick < 6:
        at_distance(tick - 2, far_step)
    if tick == 6:
        pltpu.make_async_copy(block.at[layer], line(z), own_sem).wait()
        for sz in range(Z_SIZE):
            @pl.when((sz <= z) & (z < Z_SIZE - 1))
            def _():
                remote(line(sz), line(sz), z_send.at[0, sz], z_recv.at[sz], place.to_core).wait_send()

            @pl.when((sz >= z) & (z > 0))
            def _():
                remote(line(sz), line(sz), z_send.at[1, sz], z_recv.at[sz], place.to_core).wait_send()

            for way in range(2):
                remote(line(sz), line(sz), n_send.at[way, sz], n_recv.at[way, sz], place.to_core).wait_send()
                remote(far(way, sz), far(way, sz), h_send.at[way, sz], h_recv.at[way, sz], place.to_core).wait_send()
            parts = (
                (line(sz), spot(sz, x, y, 1 - core)),
                (side(0, sz), spot(sz, 1 - x, y, 1 - core)),
                (side(1, sz), spot(sz, x, 1 - y, 1 - core)),
                (far(0, sz), spot(sz, 1 - x, 1 - y, 1 - core, 0, half)),
                (far(1, sz), spot(sz, 1 - x, 1 - y, 1 - core, half, half)),
            )
            for i, (mine, theirs) in enumerate(parts):
                remote(mine, theirs, c_send.at[i, sz], c_recv.at[i, sz], place.to_core).wait()


def all_sum(axes, values, collective):
    parts, high, wide = values.shape

    def kernel(v_ref, out_ref, box, send, recv, send2, recv2):
        place = Place(axes)
        me = place.dp * 4 + place.t
        barrier = pltpu.get_barrier_semaphore()

        def peer(i):
            other = lax.rem(me + i, parts)
            return other, (other // 4, other % 4)

        def signal(i, _):
            pl.semaphore_signal(barrier, inc=1, device_id=peer(i)[1], device_id_type=MESH)
            return 0

        lax.fori_loop(1, parts, signal, 0)
        pl.semaphore_wait(barrier, parts - 1)

        def first(i, act):
            other, device = peer(i)
            act(remote(v_ref.at[other], box.at[i], send.at[i], recv.at[i], device))
            return 0

        lax.fori_loop(1, parts, lambda i, _: first(i, lambda c: c.start()), 0)
        lax.fori_loop(1, parts, lambda i, _: first(i, lambda c: c.wait()), 0)
        out_ref[me] = v_ref[me] + jnp.sum(box[1:], axis=0)

        def second(i, act):
            other, device = peer(i)
            act(remote(out_ref.at[me], out_ref.at[me], send2.at[i], recv2.at[i], device))
            return 0

        lax.fori_loop(1, parts, lambda i, _: second(i, lambda c: c.start()), 0)

        def finish(i, _):
            other = lax.rem(me + parts - i, parts)
            c = remote(out_ref.at[me], out_ref.at[other], send2.at[i], recv2.at[i], peer(i)[1])
            c.wait()
            return 0

        lax.fori_loop(1, parts, finish, 0)

    sem = pltpu.SemaphoreType.DMA((parts,))
    return pl.pallas_call(
        kernel,
        in_specs=[pl.BlockSpec(memory_space=pltpu.VMEM)],
        out_specs=pl.BlockSpec(memory_space=pltpu.VMEM),
        out_shape=jax.ShapeDtypeStruct(values.shape, F32),
        scratch_shapes=[pltpu.VMEM(values.shape, F32), sem, sem, sem, sem],
        compiler_params=pltpu.CompilerParams(collective_id=collective, has_side_effects=True),
        name="all_sum",
    )(values)


GROUP = 4
BLOCK = 256
GROUPS = HEADS // GROUP
TOKENS = 1024
ROWS = TOKENS // SEQ
ATT_STEPS = ROWS * GROUPS
FFN_STEPS = TOKENS // BLOCK
LAYER_STEPS = ATT_STEPS + FFN_STEPS
LAYERS = 2


def norm_parts(v):
    c = v - mean_rows(v)
    r = lax.rsqrt(mean_rows(c * c) + EPS)
    return c * r, r


def attend_unit(row, grp, length, xs, w, a, b, gain, qkv_ref, u_ref, o_ref, e_ref, rinv_ref, n1_ref, r1_ref,
                n1s, bound_ref):
    here = pl.ds(pl.multiple_of(row * SEQ, SEQ), SEQ)

    @pl.when(grp == 0)
    def _():
        x = xs[here, :]
        u = dot(x, a[...]).astype(BF)
        u_ref[0] = u
        for i in range(3):
            acc = dot(x, w[WIDTH * i:WIDTH * (i + 1), :])
            if i != 1:
                acc += dot(u, b[i // 2])
            qkv_ref[0, :, WIDTH * i:WIDTH * (i + 1)] = acc.astype(BF)
        key = lax.broadcasted_iota(jnp.int32, (SEQ, 128), 0)
        bound_ref[...] = jnp.where(key < length, 3.0e38, -8.0e9)

    lane = lax.broadcasted_iota(jnp.int32, (SEQ, 128), 1)
    low = lane < HEAD_DIM
    bound = bound_ref[...]
    bound = jnp.concatenate([bound] * 4, axis=1)
    for pair in range(GROUP // 2):
        at = pl.multiple_of(grp * (GROUP * HEAD_DIM) + pair * 128, 128)
        q = qkv_ref[0, :, pl.ds(at, 128)]
        k = qkv_ref[0, :, pl.ds(WIDTH + at, 128)]
        v = qkv_ref[0, :, pl.ds(2 * WIDTH + at, 128)]
        outs = []
        for half in range(2):
            mine = low if half == 0 else ~low
            qh = jnp.where(mine, q, jnp.zeros_like(q))
            vh = jnp.where(mine, v, jnp.ones_like(v))
            s = jnp.minimum(dot_nt(k, qh), bound)
            top = jnp.max(s, axis=0, keepdims=True)
            e = jnp.exp2((s - top) * EXP2_SCALE).astype(BF)
            e_ref[0, 0, pair * 2 + half] = e
            ot = dot_tn(vh, e)
            if half == 0:
                o_t, l = ot[:HEAD_DIM], ot[HEAD_DIM:HEAD_DIM + 8]
            else:
                o_t, l = ot[HEAD_DIM:], ot[0:8]
            r = 1.0 / l
            rinv_ref[0, 0, grp * GROUP + pair * 2 + half] = r
            outs.append(o_t * r[0:1])
        both = jnp.concatenate(outs, axis=0)
        o_ref[0, :, pl.ds(at, 128)] = both.T.astype(BF)

    @pl.when(grp == GROUPS - 1)
    def _():
        m, r = norm_parts(xs[here, :].astype(F32) + dot(o_ref[0], w[3 * WIDTH:, :]))
        n1 = (m * gain).astype(BF)
        n1_ref[0] = n1
        n1s[here, :] = n1
        r1_ref[0] = jnp.broadcast_to(r, (SEQ, 128))


def ffn_unit(block, w, gain, n1s, xs, gd_ref, r2_ref):
    here = pl.ds(pl.multiple_of(block * BLOCK, BLOCK), BLOCK)
    n1 = n1s[here, :]
    f = n1.astype(F32)
    for j in range(4):
        z = dot(n1, w[j, 0])
        cdf = 0.5 + 0.5 * lax.erf(z * 0.7071067811865476)
        pdf = jnp.exp2(z * (z * (-0.5 * 1.4426950408889634))) * 0.3989422804014327
        gd_ref[0, :, CHUNK * j:CHUNK * (j + 1)] = (cdf + z * pdf).astype(BF)
        f = f + dot((z * cdf).astype(BF), w[j, 1])
    m, r = norm_parts(f)
    xs[here, :] = (m * gain).astype(BF)
    r2_ref[0] = jnp.broadcast_to(r, (BLOCK, 128))


def forward_kernel(axes, direct, len_ref, tok, att, ex, pr, a_ref, b_ref, gain_ref,
                   qkv_ref, u_ref, o_ref, e_ref, rinv_ref, n1_ref, r1_ref, gd_ref, r2_ref, xall, wat_out, wf_out,
                   xs, n1s, wat, wf, bound, x_sem, xo_sem, wa_sem, wf_sem, own_sem, *sems):
    step = pl.program_id(0)
    layer = step // LAYER_STEPS
    part = step % LAYER_STEPS
    x_in = pltpu.make_async_copy(tok, xs, x_sem.at[0])
    x_out = pltpu.make_async_copy(tok, xall.at[0], x_sem.at[1])

    def save_x(l, b):
        rows = pl.ds(pl.multiple_of(b * BLOCK, BLOCK), BLOCK)
        return pltpu.make_async_copy(xs.at[rows], xall.at[l + 1, rows], xo_sem.at[b])

    def save_attention(l):
        return pltpu.make_async_copy(wat.at[l], wat_out.at[l], wa_sem.at[l])

    def save_ffn(l):
        return pltpu.make_async_copy(wf.at[l], wf_out.at[l], wf_sem.at[l])

    def own_ffn(l):
        return [pltpu.make_async_copy(r.at[l], wf.at[l, 0, m], own_sem.at[l, m]) for m, r in enumerate((ex, pr))]

    if direct:
        place = Place(axes)
        n_att = len(ATT_SEMS)
        n_ffn = len(FFN_SEMS)
        att_sems = [sems[:n_att], sems[n_att:2 * n_att]]
        sems = sems[2 * n_att:]
        ffn_sems = [sems[:n_ffn], sems[n_ffn:]]

        def run(job):
            kind, l, tick = job
            if kind == "a":
                attention_gather(place, l, att, wat.at[l], att_sems[l], tick)
            else:
                ffn_gather(place, l, ex, pr, wf.at[l], ffn_sems[l], tick)

    @pl.when(step == 0)
    def _():
        x_in.start()
        x_out.start()
        if direct:
            greet(place, True)
            for l in range(LAYERS):
                for c in own_ffn(l):
                    c.start()
            for job in SCHEDULE[0]:
                run(job)
            for l in range(LAYERS):
                for c in own_ffn(l):
                    c.wait()
            save_attention(0).start()
        else:
            whole = [pltpu.make_async_copy(att, wat, own_sem.at[0, 0]), pltpu.make_async_copy(ex, wf, own_sem.at[0, 1])]
            for c in whole:
                c.start()
            for c in whole:
                c.wait()
        x_in.wait()

    if direct:
        for at, jobs in SCHEDULE.items():
            if at:
                @pl.when(step == at)
                def _():
                    for job in jobs:
                        run(job)
                        if job == ("a", 1, ATT_TICKS - 1):
                            save_attention(1).start()
                        if job[0] == "f" and job[2] == FFN_TICKS - 1:
                            save_ffn(job[1]).start()

    @pl.when(part < ATT_STEPS)
    def _():
        row, grp = part // GROUPS, part % GROUPS
        attend_unit(row, grp, len_ref[row], xs, wat.at[layer], a_ref.at[layer], b_ref.at[layer], gain_ref[layer, 0:1],
                    qkv_ref, u_ref, o_ref, e_ref, rinv_ref, n1_ref, r1_ref, n1s, bound)

    @pl.when(part >= ATT_STEPS)
    def _():
        block = part - ATT_STEPS

        @pl.when(layer > 0)
        def _():
            save_x(layer - 1, block).wait()

        ffn_unit(block, wf.at[layer], gain_ref[layer, 1:2], n1s, xs, gd_ref, r2_ref)
        save_x(layer, block).start()

    @pl.when(step == LAYERS * LAYER_STEPS - 1)
    def _():
        x_out.wait()
        for b in range(FFN_STEPS):
            save_x(LAYERS - 1, b).wait()
        if direct:
            for l in range(LAYERS):
                save_attention(l).wait()
                save_ffn(l).wait()


SCHEDULE = {
    0: [("a", 0, t) for t in range(5)] + [("f", 0, 0)] + [("a", 0, t) for t in range(5, 7)],
    1: [("f", 0, 1)],
    2: [("f", 0, 2)],
    3: [("f", 0, 3)],
    4: [("f", 0, 4), ("a", 1, 0)],
    5: [("f", 0, 5), ("a", 1, 1)],
    6: [("f", 0, 6), ("f", 0, 7)],
    7: [("a", 1, 2)],
    8: [("a", 1, 3)],
    9: [("a", 1, 4), ("f", 1, 0)],
    10: [("a", 1, 5), ("a", 1, 6)],
    11: [("f", 1, 1)],
    12: [("f", 1, 2)],
    13: [("f", 1, 3)],
    14: [("f", 1, 4)],
    15: [("f", 1, 5)],
    16: [("f", 1, 6), ("f", 1, 7)],
}


def forward(axes, direct, lengths, tokens, att, ex, pr, a, b, gains):
    anywhere = pl.BlockSpec(memory_space=pl.ANY)
    row_of = lambda s: jnp.minimum(s % LAYER_STEPS // GROUPS, ROWS - 1)
    block_of = lambda s: jnp.maximum(s % LAYER_STEPS - ATT_STEPS, 0)
    layer_of = lambda s: s // LAYER_STEPS
    by_row = lambda width: pl.BlockSpec((1, SEQ, width), lambda s: (layer_of(s), row_of(s), 0))
    by_block = lambda width: pl.BlockSpec((1, BLOCK, width), lambda s: (layer_of(s), block_of(s), 0))
    whole = lambda v: pl.BlockSpec(v.shape, lambda s: (0,) * v.ndim, pipeline_mode=pl.Buffered(1))
    group_of = lambda s: jnp.where(s % LAYER_STEPS < ATT_STEPS, s % LAYER_STEPS % GROUPS, GROUPS - 1)
    shape = jax.ShapeDtypeStruct
    dma = pltpu.SemaphoreType.DMA
    return pl.pallas_call(
        functools.partial(forward_kernel, axes, direct),
        grid=(LAYERS * LAYER_STEPS,),
        in_specs=[pl.BlockSpec(memory_space=pltpu.SMEM)] + [anywhere] * 4 + [whole(a), whole(b), whole(gains)],
        out_specs=[
            by_row(3 * WIDTH), by_row(2 * RANK), by_row(WIDTH),
            pl.BlockSpec((1, 1, GROUP, SEQ, SEQ), lambda s: (layer_of(s), row_of(s), group_of(s), 0, 0)),
            pl.BlockSpec((1, 1, HEADS, 8, SEQ), lambda s: (layer_of(s), row_of(s), 0, 0, 0)),
            by_row(WIDTH), by_row(128), by_block(4 * CHUNK), by_block(128), anywhere, anywhere, anywhere,
        ],
        out_shape=[
            shape((LAYERS, TOKENS, 3 * WIDTH), BF), shape((LAYERS, TOKENS, 2 * RANK), BF), shape((LAYERS, TOKENS, WIDTH), BF),
            shape((LAYERS, ROWS, HEADS, SEQ, SEQ), BF), shape((LAYERS, ROWS, HEADS, 8, SEQ), F32),
            shape((LAYERS, TOKENS, WIDTH), BF), shape((LAYERS, TOKENS, 128), F32),
            shape((LAYERS, TOKENS, 4 * CHUNK), BF), shape((LAYERS, TOKENS, 128), F32),
            shape((LAYERS + 1, TOKENS, WIDTH), BF),
            shape((LAYERS, 4 * WIDTH, WIDTH), BF), shape((LAYERS, 4, 2, WIDTH, CHUNK), BF),
        ],
        scratch_shapes=[
            pltpu.VMEM((TOKENS, WIDTH), BF), pltpu.VMEM((TOKENS, WIDTH), BF),
            pltpu.VMEM((LAYERS, 4 * WIDTH, WIDTH), BF), pltpu.VMEM((LAYERS, 4, 2, WIDTH, CHUNK), BF),
            pltpu.VMEM((SEQ, 128), F32),
            dma((2,)), dma((FFN_STEPS,)), dma((LAYERS,)), dma((LAYERS,)), dma((LAYERS, 2)),
        ] + (ATT_SEMS * 2 + FFN_SEMS * 2 if direct else []),
        compiler_params=params(1, 0 if direct else None),
        name="forward",
    )(lengths, tokens, att, ex, pr, a, b, gains)


def norm_back(e, m, r):
    return r * (e - mean_rows(e) - m * mean_rows(e * m))


def ffn_back_unit(dy, x2_ref, r2_ref, n1_ref, r1_ref, gd_ref, w, wo, gains, wait):
    g1, g2 = gains[0:1], gains[1:2]
    dh2 = norm_back(dy * g2, x2_ref[0].astype(F32) * (1.0 / g2), r2_ref[0, :, 0:1])
    df = dh2.astype(BF)
    dn = dh2
    for j in range(4):
        wait(j)
        dz = (dot_nt(df, w[j, 1]) * gd_ref[0, :, CHUNK * j:CHUNK * (j + 1)].astype(F32)).astype(BF)
        dn = dn + dot_nt(dz, w[j, 0])
    dh = norm_back(dn * g1, n1_ref[0].astype(F32) * (1.0 / g1), r1_ref[0, :, 0:1])
    wait(4)
    return dh, dot_nt(dh.astype(BF), wo[...]).astype(BF)


def attend_back_unit(grp, do_ref, qkv_ref, o_ref, e_ref, rinv_ref, d_ref):
    lane = lax.broadcasted_iota(jnp.int32, (SEQ, 128), 1)
    low = lane < HEAD_DIM
    for pair in range(GROUP // 2):
        at = pl.multiple_of(grp * (GROUP * HEAD_DIM) + pair * 128, 128)
        q = qkv_ref[0, :, pl.ds(at, 128)]
        k = qkv_ref[0, :, pl.ds(WIDTH + at, 128)]
        v = qkv_ref[0, :, pl.ds(2 * WIDTH + at, 128)]
        head = grp * GROUP + pair * 2
        scale = jnp.concatenate([rinv_ref[0, 0, head]] * 8 + [rinv_ref[0, 0, head + 1]] * 8, axis=0).T
        dos = do_ref[:, pl.ds(at, 128)].astype(F32) * scale
        other = pltpu.roll(-dos * o_ref[0, :, pl.ds(at, 128)].astype(F32), HEAD_DIM, 1).astype(BF)
        dos = dos.astype(BF)
        dvs, dks, dqs = [], [], []
        for half in range(2):
            mine = low if half == 0 else ~low
            e = e_ref[0, 0, pair * 2 + half]
            dp = dot_nt(jnp.where(mine, v, jnp.ones_like(v)), jnp.where(mine, dos, other))
            ds = (dp * e.astype(F32)).astype(BF)
            dvs.append(dot(e, dos))
            dks.append(dot(ds, q))
            dqs.append(dot_tn(k, ds)[half * HEAD_DIM:(half + 1) * HEAD_DIM])
        d_ref[:, pl.ds(2 * WIDTH + at, 128)] = jnp.where(low, dvs[0], dvs[1]).astype(BF)
        d_ref[:, pl.ds(WIDTH + at, 128)] = (jnp.where(low, dks[0], dks[1]) * HEAD_DIM ** (-0.5)).astype(BF)
        d_ref[:, pl.ds(at, 128)] = (jnp.concatenate(dqs, axis=0) * HEAD_DIM ** (-0.5)).T.astype(BF)


def backward_kernel(cot_ref, x2_ref, r2_ref, n1_ref, r1_ref, gd_ref, x_ref, u_ref, qkv_ref, o_ref, e_ref, rinv_ref,
                    a_ref, b_ref, gain_ref, wat_in, wf_in, xall,
                    dx_ref, grad_ref, hidden,
                    dhs, dos, dys, d_ref, wat, wf, wa_sem, wf_sem, h_sem):
    step = pl.program_id(0)
    layer = LAYERS - 1 - step // LAYER_STEPS
    part = step % LAYER_STEPS
    hidden_copy = pltpu.make_async_copy(xall.at[LAYERS], hidden, h_sem)

    def load_ffn(l, j):
        return pltpu.make_async_copy(wf_in.at[l, j], wf.at[j], wf_sem.at[j])

    def load_attention(l, i):
        rows = pl.ds(3 * WIDTH, WIDTH) if i == 1 else pl.ds(0, 3 * WIDTH)
        return pltpu.make_async_copy(wat_in.at[l, rows], wat.at[l, rows], wa_sem.at[l, i])

    last = LAYERS - 1

    @pl.when(step == 0)
    def _():
        for j in range(4):
            load_ffn(last, j).start()
        load_attention(last, 1).start()
        load_attention(last, 0).start()
        hidden_copy.start()
        grad_ref[...] = jnp.zeros_like(grad_ref)

    for k in range(1, LAYERS):
        @pl.when(step == k * LAYER_STEPS - ATT_STEPS)
        def _():
            for j in range(4):
                load_ffn(last - k, j).start()
            load_attention(last - k, 1).start()
            load_attention(last - k, 0).start()

        @pl.when(step == k * LAYER_STEPS)
        def _():
            for j in range(4):
                load_ffn(last - k, j).wait()
            load_attention(last - k, 1).wait()

        @pl.when(step == k * LAYER_STEPS + FFN_STEPS)
        def _():
            load_attention(last - k, 0).wait()

    @pl.when(step == FFN_STEPS)
    def _():
        load_attention(last, 0).wait()

    def ffn_part(dy, wait):
        here = pl.ds(pl.multiple_of(part * BLOCK, BLOCK), BLOCK)
        dh, do = ffn_back_unit(dy(here), x2_ref, r2_ref, n1_ref, r1_ref, gd_ref, wf, wat.at[layer, 3 * WIDTH:, :],
                               gain_ref[layer], wait)
        dhs[here, :] = dh
        dos[here, :] = do

    def wait_load(j):
        if j < 4:
            load_ffn(last, j).wait()
        else:
            load_attention(last, 1).wait()

    @pl.when(step == 0)
    def _():
        ffn_part(lambda here: cot_ref[...].astype(F32), wait_load)

    @pl.when((step > 0) & (step < FFN_STEPS))
    def _():
        ffn_part(lambda here: cot_ref[...].astype(F32), lambda j: None)

    @pl.when((step >= LAYER_STEPS) & (part < FFN_STEPS))
    def _():
        ffn_part(lambda here: dys[here, :], lambda j: None)

    @pl.when(part >= FFN_STEPS)
    def _():
        row, grp = (part - FFN_STEPS) // GROUPS, (part - FFN_STEPS) % GROUPS
        here = pl.ds(pl.multiple_of(row * SEQ, SEQ), SEQ)
        attend_back_unit(grp, dos.at[here], qkv_ref, o_ref, e_ref, rinv_ref, d_ref)

        @pl.when(grp == GROUPS - 1)
        def _():
            dq, dk, dv = (d_ref[:, WIDTH * i:WIDTH * (i + 1)] for i in range(3))
            du = (dot_nt(dq, b_ref[layer, 0]) + dot_nt(dv, b_ref[layer, 1])).astype(BF)
            u = u_ref[0]
            u2 = u + u
            ga = dot_tn(du, x_ref[0])
            gq = dot_tn(u2, dq)[:RANK]
            gv = dot_tn(u2, dv)[RANK:]
            grad_ref[layer] += jnp.concatenate([ga, gq, gv], axis=0)
            w = wat.at[layer]
            dx = (dhs[here, :] + dot_nt(dq, w[0:WIDTH, :]) + dot_nt(dk, w[WIDTH:2 * WIDTH, :])
                  + dot_nt(dv, w[2 * WIDTH:3 * WIDTH, :]) + dot_nt(du, a_ref[layer]))

            @pl.when(layer > 0)
            def _():
                dys[here, :] = dx

            @pl.when(layer == 0)
            def _():
                dx_ref[...] = dx

    @pl.when(step == LAYERS * LAYER_STEPS - 1)
    def _():
        hidden_copy.wait()


def backward(cot, saved, a, b, gains, wat, wf):
    qkv, u, o, e, rinv, n1, r1, gd, r2, xall = saved
    anywhere = pl.BlockSpec(memory_space=pl.ANY)
    layer_of = lambda s: LAYERS - 1 - s // LAYER_STEPS
    block_of = lambda s: jnp.minimum(s % LAYER_STEPS, FFN_STEPS - 1)
    unit_of = lambda s: jnp.maximum(s % LAYER_STEPS - FFN_STEPS, 0)
    row_of = lambda s: unit_of(s) // GROUPS
    group_of = lambda s: unit_of(s) % GROUPS
    by_row = lambda width: pl.BlockSpec((1, SEQ, width), lambda s: (layer_of(s), row_of(s), 0))
    by_block = lambda width: pl.BlockSpec((1, BLOCK, width), lambda s: (layer_of(s), block_of(s), 0))
    whole = lambda v: pl.BlockSpec(v.shape, lambda s: (0,) * v.ndim, pipeline_mode=pl.Buffered(1))
    shape = jax.ShapeDtypeStruct
    dma = pltpu.SemaphoreType.DMA
    return pl.pallas_call(
        backward_kernel,
        grid=(LAYERS * LAYER_STEPS,),
        in_specs=[
            pl.BlockSpec((BLOCK, WIDTH), lambda s: (jnp.minimum(s, FFN_STEPS - 1), 0)),
            pl.BlockSpec((1, BLOCK, WIDTH), lambda s: (layer_of(s) + 1, block_of(s), 0)),
            by_block(128), by_block(WIDTH), by_block(128), by_block(4 * CHUNK),
            by_row(WIDTH), by_row(2 * RANK), by_row(3 * WIDTH), by_row(WIDTH),
            pl.BlockSpec((1, 1, GROUP, SEQ, SEQ), lambda s: (layer_of(s), row_of(s), group_of(s), 0, 0)),
            pl.BlockSpec((1, 1, HEADS, 8, SEQ), lambda s: (layer_of(s), row_of(s), 0, 0, 0)),
            whole(a), whole(b), whole(gains), anywhere, anywhere, anywhere,
        ],
        out_specs=[
            pl.BlockSpec((SEQ, WIDTH), lambda s: (jnp.where(s < LAYER_STEPS * (LAYERS - 1), 0, row_of(s)), 0)),
            pl.BlockSpec((LAYERS, 4 * RANK, WIDTH), lambda s: (0, 0, 0)),
            anywhere,
        ],
        out_shape=[shape((TOKENS, WIDTH), F32), shape((LAYERS, 4 * RANK, WIDTH), F32), shape((TOKENS, WIDTH), BF)],
        scratch_shapes=[
            pltpu.VMEM((TOKENS, WIDTH), F32), pltpu.VMEM((TOKENS, WIDTH), BF), pltpu.VMEM((TOKENS, WIDTH), F32),
            pltpu.VMEM((SEQ, 3 * WIDTH), BF), pltpu.VMEM((LAYERS, 4 * WIDTH, WIDTH), BF),
            pltpu.VMEM((4, 2, WIDTH, CHUNK), BF),
            dma((LAYERS, 2)), dma((4,)), dma,
        ],
        compiler_params=params(1),
        name="backward",
    )(cot, xall, r2, n1, r1, gd, xall, u, qkv, o, e, rinv, a, b, gains, wat, wf, xall)


def local(axes, direct, tokens, lengths, attention, down, up, expand, project, gains, cotangent):
    a = jnp.concatenate([down[:, 0], down[:, 1]], axis=2)
    twice = up + up
    b = jnp.stack([jnp.pad(twice[:, 0], ((0, 0), (0, RANK), (0, 0))), jnp.pad(twice[:, 1], ((0, 0), (RANK, 0), (0, 0)))],
                  axis=1)
    if direct:
        att, ex, pr = attention, expand, project
    else:
        att = lax.all_gather(attention, axes, axis=1, tiled=True)
        w1 = lax.all_gather(expand, axes[1], axis=2, tiled=True).reshape(LAYERS, WIDTH, 4, CHUNK).transpose(0, 2, 1, 3)
        w2 = lax.all_gather(project, axes[1], axis=1, tiled=True).reshape(LAYERS, 4, CHUNK, WIDTH)
        ex = pr = jnp.stack([w1, w2], axis=2)
    *saved, wat, wf = forward(axes, direct, lengths, tokens, att, ex, pr, a, b, gains)
    if not direct:
        wat, wf = att, ex
    dx, grads, hidden = backward(cotangent, saved, a, b, gains, wat, wf)
    if direct:
        total = all_sum(axes, grads.reshape(32, -1, 128), 1).reshape(grads.shape)
    else:
        total = lax.psum(grads, axes)
    a_grad = total[:, :2 * RANK].reshape(LAYERS, 2, RANK, WIDTH).transpose(0, 1, 3, 2)
    b_grad = total[:, 2 * RANK:].reshape(LAYERS, 2, RANK, WIDTH)
    return hidden, dx, a_grad, b_grad


def solution(mesh):
    axes = tuple(mesh.axis_names)
    dp, tensor = axes
    direct = mesh.shape[dp] == 2 * Z_SIZE and mesh.shape[tensor] == 4
    placed = (
        P(axes, None), P(axes), P(None, axes, None), P(), P(),
        P(None, None, tensor), P(None, tensor, None), P(), P(axes, None),
    )
    return jax.shard_map(
        functools.partial(local, axes, direct),
        mesh=mesh,
        in_specs=placed,
        out_specs=(P(axes, None), P(axes, None), P(), P()),
        check_vma=False,
    )
```

profile of v0, /device:TPU:0, one launch (start us, length us, event | category | flops | bytes accessed | tf_op | source)
XLA Modules:
  0.0 245.1 jit_solution(12863975941337494113)
XLA Ops:
  0.6 0.8 copy_add_fusion
  1.5 0.7 pad_maximum_fusion.b_ref
  2.1 0.8 slice_bitcast_fusion.5
  2.9 0.9 copy.28.a_ref
  3.8 132.8 %forward.1 = (bf16[2,1024,2304]{2,1,0:T(8,128)(2,1)}, bf16[2,1024,16]{2,1,0:T(8,128)(2,1)}, bf16[2,1024,768]{2,1,0:T(8,128)(2,1)}, bf16[2,2,12,512,512]{4,3,2,1,...) custom-call(s32[2]{0:T(128)} %len_ref.1, ...), custom_call_target="tpu_custom_call" | custom-call | tf_op jit(solution)/shard_map/forward/pallas_call | solution.py:563
  136.6 85.8 %backward.1 = (f32[1024,768]{1,0:T(8,128)}, f32[2,32,768]{2,1,0:T(8,128)}, bf16[1024,768]{1,0:T(8,128)(2,1)}) custom-call(bf16[1024,768]{1,0:T(8,128)(2,1)} %cot_ref.1, bf16[3,1024,768]{2,1,0:T(8,128)(2,1)} %get-tuple-element.19.x2_ref.x_ref.xall, f32[2,1024,128]{2,1,0:T(8,128)} %get-tuple-element.20.r2_ref, bf16[2,1024,768]{2,1,0:T(8,128)(2,1)} %get-tuple-element.21.n1_ref, ...), custom_call_target="tpu_custom_call" | custom-call | tf_op jit(solution)/shard_map/backward/pallas_call | solution.py:757
  222.4 1.7 reshape.20.v_ref
  224.1 19.3 %all_sum.1 = f32[32,12,128]{2,1,0:T(8,128)} custom-call(f32[32,12,128]{2,1,0:T(8,128)} %reshape.20.v_ref), custom_call_target="tpu_custom_call" | custom-call | tf_op jit(solution)/shard_map/all_sum/pallas_call | solution.py:333
  243.4 1.0 reshape.21
  244.4 0.7 slice_bitcast_fusion
  (3 shorter events, 0.0 us)
where the time goes:
time: 245 us
  Pallas kernels  238 us (97%)
  local copies, waits for them, and re-layouts  5.06 us (2%)
    pallas_call x1, Pallas kernels, forward(): pl.pallas_call(functools.partial(forward_kernel, axes, direct), grid=(LAY...  133 us
    pallas_call x1, Pallas kernels, backward(): pl.pallas_call(backward_kernel, grid=(LAYERS * LAYER_STEPS,), in_specs=[p...  85.8 us
    pallas_call x1, Pallas kernels, all_sum(): pl.pallas_call(kernel, in_specs=[pl.BlockSpec(memory_space=pltpu.VMEM)],...  19.3 us

commit v1 on v0

--- a/solution.py
+++ b/solution.py
@@ -100,10 +100,9 @@
     pltpu.SemaphoreType.DMA((14,)),
     pltpu.SemaphoreType.DMA((14,)),
 ]
-FFN_TICKS = 8
-
-
-def ffn_gather(place, layer, w1, w2, out, sems, tick):
+
+
+def ffn_gather(place, layer, w1, w2, out, sems, what, tick=0):
     send, recv, core_send, core_recv = sems
     g = place.x * 2 + place.z % 2
     gd = 3 - g
@@ -132,12 +131,12 @@
     def share(s):
         remote(spot(1, s), spot(2, s), core_send.at[s], core_recv.at[s], place.to_core).start()
 
-    if tick == 0:
-        for i in range(4):
-            over_y(i)
+    if what == "fy":
+        over_y(tick)
+    elif what == "fown":
         for m, ref in enumerate((w1, w2)):
             remote(ref.at[layer], out.at[1, m], core_send.at[12 + m], core_recv.at[12 + m], place.to_core).start()
-    elif tick < 4:
+    elif what == "fr" and tick < 4:
         s = 3 * g + tick - 1
         arrived(s)
         over(1, tick - 1, s)
@@ -147,7 +146,7 @@
             for s in (3 * gx, 3 * gz):
                 arrived(s)
                 share(s)
-    elif tick == 4:
+    elif what == "fr" and tick == 4:
         s = 3 * gz + 1
         arrived(s)
         over(1, 3, s)
@@ -155,7 +154,7 @@
         for s in (3 * gd, 3 * gx + 1):
             arrived(s)
             share(s)
-    elif tick == 5:
+    elif what == "fr" and tick == 5:
         s = 3 * gx + 2
         arrived(s)
         over(2, 3, s)
@@ -163,7 +162,7 @@
         s = 3 * gz + 2
         arrived(s)
         share(s)
-    elif tick == 6:
+    elif what == "fr" and tick == 6:
         for s in (3 * gd + 1, 3 * gd + 2):
             arrived(s)
             share(s)
@@ -188,14 +187,14 @@
     pltpu.SemaphoreType.DMA((5, 4)),
     pltpu.SemaphoreType.DMA,
 ]
-ATT_TICKS = 7
-
-
-def attention_gather(place, layer, block, out, sems, tick):
+
+
+def attention_gather(place, layer, block, out, sems, what, d=0):
     z_send, z_recv, n_send, n_recv, h_send, h_recv, c_send, c_recv, own_sem = sems
     rows = block.shape[1]
     half = rows // 2
     z, x, y, core = place.z, place.x, place.y, place.core
+    late = Z_SIZE - 1
 
     def spot(sz, sx, sy, sc, start=0, size=rows):
         at = ((sz * 2 + sx) * 4 + sy * 2 + sc) * rows + start
@@ -212,15 +211,19 @@
 
     devices = (place.to_x, place.to_y)
 
-    def at_distance(d, action):
+    def at_distance(d, action, size):
         if d == 0:
-            action(z)
+            @pl.when(z < size)
+            def _():
+                action(z)
+
             return
+
         @pl.when(z >= d)
         def _():
             action(z - d)
 
-        @pl.when(z + d < Z_SIZE)
+        @pl.when(z + d < size)
         def _():
             action(z + d)
 
@@ -237,6 +240,16 @@
         def _():
             remote(mine, line(sz), z_send.at[1, sz], z_recv.at[sz], place.to_down).start()
 
+        if own:
+            @pl.when(sz < late)
+            def _():
+                spread(sz, mine)
+        else:
+            @pl.when(sz < late)
+            def _():
+                spread(sz, line(sz))
+
+    def spread(sz, mine):
         for way in range(2):
             remote(mine, line(sz), n_send.at[way, sz], n_recv.at[way, sz], devices[way]).start()
         remote(mine, line(sz), c_send.at[0, sz], c_recv.at[0, sz], place.to_core).start()
@@ -253,37 +266,55 @@
             remote(far(way, sz), far(way, sz), h_send.at[way, sz], h_recv.at[way, sz], place.to_core).wait_recv()
             remote(far(way, sz), far(way, sz), c_send.at[3 + way, sz], c_recv.at[3 + way, sz], place.to_core).start()
 
-    if tick == 0:
-        pltpu.make_async_copy(block.at[layer], line(z), own_sem).start()
-    if tick < 4:
-        at_distance(tick, functools.partial(line_step, own=tick == 0))
-    if 1 <= tick < 5:
-        at_distance(tick - 1, side_step)
-    if 2 <= tick < 6:
-        at_distance(tick - 2, far_step)
-    if tick == 6:
-        pltpu.make_async_copy(block.at[layer], line(z), own_sem).wait()
-        for sz in range(Z_SIZE):
-            @pl.when((sz <= z) & (z < Z_SIZE - 1))
-            def _():
-                remote(line(sz), line(sz), z_send.at[0, sz], z_recv.at[sz], place.to_core).wait_send()
-
-            @pl.when((sz >= z) & (z > 0))
-            def _():
-                remote(line(sz), line(sz), z_send.at[1, sz], z_recv.at[sz], place.to_core).wait_send()
-
-            for way in range(2):
-                remote(line(sz), line(sz), n_send.at[way, sz], n_recv.at[way, sz], place.to_core).wait_send()
-                remote(far(way, sz), far(way, sz), h_send.at[way, sz], h_recv.at[way, sz], place.to_core).wait_send()
-            parts = (
-                (line(sz), spot(sz, x, y, 1 - core)),
-                (side(0, sz), spot(sz, 1 - x, y, 1 - core)),
-                (side(1, sz), spot(sz, x, 1 - y, 1 - core)),
-                (far(0, sz), spot(sz, 1 - x, 1 - y, 1 - core, 0, half)),
-                (far(1, sz), spot(sz, 1 - x, 1 - y, 1 - core, half, half)),
-            )
-            for i, (mine, theirs) in enumerate(parts):
-                remote(mine, theirs, c_send.at[i, sz], c_recv.at[i, sz], place.to_core).wait()
+    def finish(sz):
+        @pl.when((sz <= z) & (z < Z_SIZE - 1))
+        def _():
+            remote(line(sz), line(sz), z_send.at[0, sz], z_recv.at[sz], place.to_core).wait_send()
+
+        @pl.when((sz >= z) & (z > 0))
+        def _():
+            remote(line(sz), line(sz), z_send.at[1, sz], z_recv.at[sz], place.to_core).wait_send()
+
+        for way in range(2):
+            remote(line(sz), line(sz), n_send.at[way, sz], n_recv.at[way, sz], place.to_core).wait_send()
+            remote(far(way, sz), far(way, sz), h_send.at[way, sz], h_recv.at[way, sz], place.to_core).wait_send()
+        parts = (
+            (line(sz), spot(sz, x, y, 1 - core)),
+            (side(0, sz), spot(sz, 1 - x, y, 1 - core)),
+            (side(1, sz), spot(sz, x, 1 - y, 1 - core)),
+            (far(0, sz), spot(sz, 1 - x, 1 - y, 1 - core, 0, half)),
+            (far(1, sz), spot(sz, 1 - x, 1 - y, 1 - core, half, half)),
+        )
+        for i, (mine, theirs) in enumerate(parts):
+            remote(mine, theirs, c_send.at[i, sz], c_recv.at[i, sz], place.to_core).wait()
+
+    own_copy = pltpu.make_async_copy(block.at[layer], line(z), own_sem)
+    if what == "line":
+        if d == 0:
+            own_copy.start()
+        at_distance(d, functools.partial(line_step, own=d == 0), Z_SIZE)
+    if what == "side":
+        at_distance(d, side_step, late)
+    if what == "far":
+        at_distance(d, far_step, late)
+    if what == "fin012":
+        own_copy.wait()
+        for sz in range(late):
+            finish(sz)
+    if what == "line3":
+        @pl.when(z == late)
+        def _():
+            spread(late, block.at[layer])
+
+        @pl.when(z < late)
+        def _():
+            spread(late, line(late))
+    if what == "side3":
+        side_step(late)
+    if what == "far3":
+        far_step(late)
+    if what == "fin3":
+        finish(late)
 
 
 def all_sum(axes, values, collective):
@@ -341,7 +372,7 @@
     )(values)
 
 
-GROUP = 4
+GROUP = 6
 BLOCK = 256
 GROUPS = HEADS // GROUP
 TOKENS = 1024
@@ -349,6 +380,7 @@
 ATT_STEPS = ROWS * GROUPS
 FFN_STEPS = TOKENS // BLOCK
 LAYER_STEPS = ATT_STEPS + FFN_STEPS
+FORWARD_STEPS = ROWS + FFN_STEPS
 LAYERS = 2
 
 
@@ -358,32 +390,27 @@
     return c * r, r
 
 
-def attend_unit(row, grp, length, xs, w, a, b, gain, qkv_ref, u_ref, o_ref, e_ref, rinv_ref, n1_ref, r1_ref,
-                n1s, bound_ref):
+def attend_unit(row, length, xs, w, a, b, gain, qkv_ref, u_ref, o_ref, e_ref, rinv_ref, n1_ref, r1_ref, n1s, slot):
     here = pl.ds(pl.multiple_of(row * SEQ, SEQ), SEQ)
-
-    @pl.when(grp == 0)
-    def _():
-        x = xs[here, :]
-        u = dot(x, a[...]).astype(BF)
-        u_ref[0] = u
-        for i in range(3):
-            acc = dot(x, w[WIDTH * i:WIDTH * (i + 1), :])
-            if i != 1:
-                acc += dot(u, b[i // 2])
-            qkv_ref[0, :, WIDTH * i:WIDTH * (i + 1)] = acc.astype(BF)
-        key = lax.broadcasted_iota(jnp.int32, (SEQ, 128), 0)
-        bound_ref[...] = jnp.where(key < length, 3.0e38, -8.0e9)
-
+    x = xs[here, :]
+    u = dot(x, a[...]).astype(BF)
+    u_ref[0] = u
+    for i in range(3):
+        acc = dot(x, w[WIDTH * i:WIDTH * (i + 1), :])
+        if i != 1:
+            acc += dot(u, b[i // 2])
+        qkv_ref[0, :, WIDTH * i:WIDTH * (i + 1)] = acc.astype(BF)
+    key = lax.broadcasted_iota(jnp.int32, (SEQ, 128), 0)
+    bound = jnp.where(key < length, 3.0e38, -8.0e9)
     lane = lax.broadcasted_iota(jnp.int32, (SEQ, 128), 1)
     low = lane < HEAD_DIM
-    bound = bound_ref[...]
     bound = jnp.concatenate([bound] * 4, axis=1)
-    for pair in range(GROUP // 2):
-        at = pl.multiple_of(grp * (GROUP * HEAD_DIM) + pair * 128, 128)
-        q = qkv_ref[0, :, pl.ds(at, 128)]
-        k = qkv_ref[0, :, pl.ds(WIDTH + at, 128)]
-        v = qkv_ref[0, :, pl.ds(2 * WIDTH + at, 128)]
+    for pair in range(HEADS // 2):
+        slot(pair)
+        at = pair * 128
+        q = qkv_ref[0, :, at:at + 128]
+        k = qkv_ref[0, :, WIDTH + at:WIDTH + at + 128]
+        v = qkv_ref[0, :, 2 * WIDTH + at:2 * WIDTH + at + 128]
         outs = []
         for half in range(2):
             mine = low if half == 0 else ~low
@@ -399,18 +426,16 @@
             else:
                 o_t, l = ot[HEAD_DIM:], ot[0:8]
             r = 1.0 / l
-            rinv_ref[0, 0, grp * GROUP + pair * 2 + half] = r
+            rinv_ref[0, 0, pair * 2 + half] = r
             outs.append(o_t * r[0:1])
         both = jnp.concatenate(outs, axis=0)
-        o_ref[0, :, pl.ds(at, 128)] = both.T.astype(BF)
-
-    @pl.when(grp == GROUPS - 1)
-    def _():
-        m, r = norm_parts(xs[here, :].astype(F32) + dot(o_ref[0], w[3 * WIDTH:, :]))
-        n1 = (m * gain).astype(BF)
-        n1_ref[0] = n1
-        n1s[here, :] = n1
-        r1_ref[0] = jnp.broadcast_to(r, (SEQ, 128))
+        o_ref[0, :, at:at + 128] = both.T.astype(BF)
+    slot(HEADS // 2)
+    m, r = norm_parts(xs[here, :].astype(F32) + dot(o_ref[0], w[3 * WIDTH:, :]))
+    n1 = (m * gain).astype(BF)
+    n1_ref[0] = n1
+    n1s[here, :] = n1
+    r1_ref[0] = jnp.broadcast_to(r, (SEQ, 128))
 
 
 def ffn_unit(block, w, gain, n1s, xs, gd_ref, r2_ref):
@@ -430,12 +455,11 @@
 
 def forward_kernel(axes, direct, len_ref, tok, att, ex, pr, a_ref, b_ref, gain_ref,
                    qkv_ref, u_ref, o_ref, e_ref, rinv_ref, n1_ref, r1_ref, gd_ref, r2_ref, xall, wat_out, wf_out,
-                   xs, n1s, wat, wf, bound, x_sem, xo_sem, wa_sem, wf_sem, own_sem, *sems):
-    step = pl.program_id(0)
-    layer = step // LAYER_STEPS
-    part = step % LAYER_STEPS
+                   xs, n1s, wat, wf, x_sem, xo_sem, wa_sem, wf_sem, own_sem, *sems):
+    layer, part = pl.program_id(0), pl.program_id(1)
+    step = layer * FORWARD_STEPS + part
     x_in = pltpu.make_async_copy(tok, xs, x_sem.at[0])
-    x_out = pltpu.make_async_copy(tok, xall.at[0], x_sem.at[1])
+    x_out = pltpu.make_async_copy(xs, xall.at[0], x_sem.at[1])
 
     def save_x(l, b):
         rows = pl.ds(pl.multiple_of(b * BLOCK, BLOCK), BLOCK)
@@ -459,27 +483,29 @@
         ffn_sems = [sems[:n_ffn], sems[n_ffn:]]
 
         def run(job):
-            kind, l, tick = job
-            if kind == "a":
-                attention_gather(place, l, att, wat.at[l], att_sems[l], tick)
+            what, l, *more = job
+            if what in ("fy", "fown", "fr", "ffin"):
+                ffn_gather(place, l, ex, pr, wf.at[l], ffn_sems[l], what, *more)
             else:
-                ffn_gather(place, l, ex, pr, wf.at[l], ffn_sems[l], tick)
+                attention_gather(place, l, att, wat.at[l], att_sems[l], what, *more)
+            if what == "fin3":
+                save_attention(l).start()
+            if what == "ffin":
+                save_ffn(l).start()
 
     @pl.when(step == 0)
     def _():
         x_in.start()
-        x_out.start()
         if direct:
             greet(place, True)
             for l in range(LAYERS):
                 for c in own_ffn(l):
                     c.start()
-            for job in SCHEDULE[0]:
+            for job in SCHEDULE[0, 0]:
                 run(job)
             for l in range(LAYERS):
                 for c in own_ffn(l):
                     c.wait()
-            save_attention(0).start()
         else:
             whole = [pltpu.make_async_copy(att, wat, own_sem.at[0, 0]), pltpu.make_async_copy(ex, wf, own_sem.at[0, 1])]
             for c in whole:
@@ -487,28 +513,30 @@
             for c in whole:
                 c.wait()
         x_in.wait()
-
-    if direct:
-        for at, jobs in SCHEDULE.items():
-            if at:
+        x_out.start()
+
+    def slot(within):
+        for (at, where), jobs in SCHEDULE.items():
+            if direct and where == within and (at, where) != (0, 0):
                 @pl.when(step == at)
                 def _():
                     for job in jobs:
                         run(job)
-                        if job == ("a", 1, ATT_TICKS - 1):
-                            save_attention(1).start()
-                        if job[0] == "f" and job[2] == FFN_TICKS - 1:
-                            save_ffn(job[1]).start()
-
-    @pl.when(part < ATT_STEPS)
-    def _():
-        row, grp = part // GROUPS, part % GROUPS
-        attend_unit(row, grp, len_ref[row], xs, wat.at[layer], a_ref.at[layer], b_ref.at[layer], gain_ref[layer, 0:1],
-                    qkv_ref, u_ref, o_ref, e_ref, rinv_ref, n1_ref, r1_ref, n1s, bound)
-
-    @pl.when(part >= ATT_STEPS)
-    def _():
-        block = part - ATT_STEPS
+
+    slot(0)
+
+    @pl.when(part < ROWS)
+    def _():
+        attend_unit(part, len_ref[part], xs, wat.at[layer], a_ref.at[layer], b_ref.at[layer], gain_ref[layer, 0:1],
+                    qkv_ref, u_ref, o_ref, e_ref, rinv_ref, n1_ref, r1_ref, n1s, lambda pair: slot(pair) if pair else None)
+
+    @pl.when(part >= ROWS)
+    def _():
+        block = part - ROWS
+
+        @pl.when(step == ROWS)
+        def _():
+            x_out.wait()
 
         @pl.when(layer > 0)
         def _():
@@ -517,9 +545,8 @@
         ffn_unit(block, wf.at[layer], gain_ref[layer, 1:2], n1s, xs, gd_ref, r2_ref)
         save_x(layer, block).start()
 
-    @pl.when(step == LAYERS * LAYER_STEPS - 1)
-    def _():
-        x_out.wait()
+    @pl.when(step == LAYERS * FORWARD_STEPS - 1)
+    def _():
         for b in range(FFN_STEPS):
             save_x(LAYERS - 1, b).wait()
         if direct:
@@ -529,45 +556,72 @@
 
 
 SCHEDULE = {
-    0: [("a", 0, t) for t in range(5)] + [("f", 0, 0)] + [("a", 0, t) for t in range(5, 7)],
-    1: [("f", 0, 1)],
-    2: [("f", 0, 2)],
-    3: [("f", 0, 3)],
-    4: [("f", 0, 4), ("a", 1, 0)],
-    5: [("f", 0, 5), ("a", 1, 1)],
-    6: [("f", 0, 6), ("f", 0, 7)],
-    7: [("a", 1, 2)],
-    8: [("a", 1, 3)],
-    9: [("a", 1, 4), ("f", 1, 0)],
-    10: [("a", 1, 5), ("a", 1, 6)],
-    11: [("f", 1, 1)],
-    12: [("f", 1, 2)],
-    13: [("f", 1, 3)],
-    14: [("f", 1, 4)],
-    15: [("f", 1, 5)],
-    16: [("f", 1, 6), ("f", 1, 7)],
+    (0, 0): [
+        ("line", 0, 0), ("fy", 0, 0), ("line", 0, 1), ("fr", 0, 1), ("fy", 0, 1), ("line", 0, 2),
+        ("side", 0, 0), ("side", 0, 1), ("side", 0, 2), ("fown", 0), ("line", 0, 3), ("line3", 0),
+        ("side", 0, 3), ("line", 1, 0), ("fy", 0, 2), ("fr", 0, 2), ("fy", 0, 3), ("far", 0, 0),
+        ("far", 0, 1), ("far", 0, 2), ("far", 0, 3), ("side3", 0), ("fin012", 0), ("line", 1, 1),
+        ("line", 1, 2),
+    ],
+    (0, 2): [
+        ("fr", 0, 3), ("side", 1, 0), ("far3", 0), ("line", 1, 3),
+    ],
+    (0, 4): [
+        ("fin3", 0),
+    ],
+    (1, 0): [
+        ("fr", 0, 4), ("fy", 1, 0), ("fr", 0, 5), ("fy", 1, 1), ("fown", 1),
+    ],
+    (1, 2): [
+        ("side", 1, 1), ("side", 1, 2), ("line3", 1), ("far", 1, 0),
+    ],
+    (1, 4): [
+        ("fr", 0, 6), ("fr", 1, 1), ("side", 1, 3),
+    ],
+    (2, 0): [
+        ("fr", 1, 2), ("ffin", 0),
+    ],
+    (3, 0): [
+        ("fy", 1, 2),
+    ],
+    (5, 0): [
+        ("far", 1, 1), ("side3", 1), ("far", 1, 2), ("fy", 1, 3), ("far", 1, 3),
+    ],
+    (6, 0): [
+        ("fr", 1, 3), ("fin012", 1),
+    ],
+    (6, 2): [
+        ("far3", 1),
+    ],
+    (6, 4): [
+        ("fin3", 1), ("fr", 1, 4), ("fr", 1, 5),
+    ],
+    (7, 2): [
+        ("fr", 1, 6),
+    ],
+    (8, 0): [
+        ("ffin", 1),
+    ],
 }
 
 
 def forward(axes, direct, lengths, tokens, att, ex, pr, a, b, gains):
     anywhere = pl.BlockSpec(memory_space=pl.ANY)
-    row_of = lambda s: jnp.minimum(s % LAYER_STEPS // GROUPS, ROWS - 1)
-    block_of = lambda s: jnp.maximum(s % LAYER_STEPS - ATT_STEPS, 0)
-    layer_of = lambda s: s // LAYER_STEPS
-    by_row = lambda width: pl.BlockSpec((1, SEQ, width), lambda s: (layer_of(s), row_of(s), 0))
-    by_block = lambda width: pl.BlockSpec((1, BLOCK, width), lambda s: (layer_of(s), block_of(s), 0))
-    whole = lambda v: pl.BlockSpec(v.shape, lambda s: (0,) * v.ndim, pipeline_mode=pl.Buffered(1))
-    group_of = lambda s: jnp.where(s % LAYER_STEPS < ATT_STEPS, s % LAYER_STEPS % GROUPS, GROUPS - 1)
+    row_of = lambda p: jnp.minimum(p, ROWS - 1)
+    block_of = lambda p: jnp.maximum(p - ROWS, 0)
+    by_row = lambda width: pl.BlockSpec((1, SEQ, width), lambda l, p: (l, row_of(p), 0))
+    by_block = lambda width: pl.BlockSpec((1, BLOCK, width), lambda l, p: (l, block_of(p), 0))
+    whole = lambda v: pl.BlockSpec(v.shape, lambda l, p: (0,) * v.ndim, pipeline_mode=pl.Buffered(1))
     shape = jax.ShapeDtypeStruct
     dma = pltpu.SemaphoreType.DMA
     return pl.pallas_call(
         functools.partial(forward_kernel, axes, direct),
-        grid=(LAYERS * LAYER_STEPS,),
+        grid=(LAYERS, FORWARD_STEPS),
         in_specs=[pl.BlockSpec(memory_space=pltpu.SMEM)] + [anywhere] * 4 + [whole(a), whole(b), whole(gains)],
         out_specs=[
             by_row(3 * WIDTH), by_row(2 * RANK), by_row(WIDTH),
-            pl.BlockSpec((1, 1, GROUP, SEQ, SEQ), lambda s: (layer_of(s), row_of(s), group_of(s), 0, 0)),
-            pl.BlockSpec((1, 1, HEADS, 8, SEQ), lambda s: (layer_of(s), row_of(s), 0, 0, 0)),
+            pl.BlockSpec((1, 1, HEADS, SEQ, SEQ), lambda l, p: (l, row_of(p), 0, 0, 0)),
+            pl.BlockSpec((1, 1, HEADS, 8, SEQ), lambda l, p: (l, row_of(p), 0, 0, 0)),
             by_row(WIDTH), by_row(128), by_block(4 * CHUNK), by_block(128), anywhere, anywhere, anywhere,
         ],
         out_shape=[
@@ -581,10 +635,9 @@
         scratch_shapes=[
             pltpu.VMEM((TOKENS, WIDTH), BF), pltpu.VMEM((TOKENS, WIDTH), BF),
             pltpu.VMEM((LAYERS, 4 * WIDTH, WIDTH), BF), pltpu.VMEM((LAYERS, 4, 2, WIDTH, CHUNK), BF),
-            pltpu.VMEM((SEQ, 128), F32),
             dma((2,)), dma((FFN_STEPS,)), dma((LAYERS,)), dma((LAYERS,)), dma((LAYERS, 2)),
         ] + (ATT_SEMS * 2 + FFN_SEMS * 2 if direct else []),
-        compiler_params=params(1, 0 if direct else None),
+        compiler_params=params(2, 0 if direct else None),
         name="forward",
     )(lengths, tokens, att, ex, pr, a, b, gains)
 
@@ -634,13 +687,18 @@
         d_ref[:, pl.ds(at, 128)] = (jnp.concatenate(dqs, axis=0) * HEAD_DIM ** (-0.5)).T.astype(BF)
 
 
+def split(unit):
+    row = sum(jnp.where(unit >= GROUPS * r, 1, 0) for r in range(1, ROWS))
+    return row, unit - row * GROUPS
+
+
 def backward_kernel(cot_ref, x2_ref, r2_ref, n1_ref, r1_ref, gd_ref, x_ref, u_ref, qkv_ref, o_ref, e_ref, rinv_ref,
                     a_ref, b_ref, gain_ref, wat_in, wf_in, xall,
                     dx_ref, grad_ref, hidden,
                     dhs, dos, dys, d_ref, wat, wf, wa_sem, wf_sem, h_sem):
-    step = pl.program_id(0)
-    layer = LAYERS - 1 - step // LAYER_STEPS
-    part = step % LAYER_STEPS
+    turn, part = pl.program_id(0), pl.program_id(1)
+    layer = LAYERS - 1 - turn
+    step = turn * LAYER_STEPS + part
     hidden_copy = pltpu.make_async_copy(xall.at[LAYERS], hidden, h_sem)
 
     def load_ffn(l, j):
@@ -710,7 +768,7 @@
 
     @pl.when(part >= FFN_STEPS)
     def _():
-        row, grp = (part - FFN_STEPS) // GROUPS, (part - FFN_STEPS) % GROUPS
+        row, grp = split(part - FFN_STEPS)
         here = pl.ds(pl.multiple_of(row * SEQ, SEQ), SEQ)
         attend_back_unit(grp, dos.at[here], qkv_ref, o_ref, e_ref, rinv_ref, d_ref)
 
@@ -744,31 +802,30 @@
 def backward(cot, saved, a, b, gains, wat, wf):
     qkv, u, o, e, rinv, n1, r1, gd, r2, xall = saved
     anywhere = pl.BlockSpec(memory_space=pl.ANY)
-    layer_of = lambda s: LAYERS - 1 - s // LAYER_STEPS
-    block_of = lambda s: jnp.minimum(s % LAYER_STEPS, FFN_STEPS - 1)
-    unit_of = lambda s: jnp.maximum(s % LAYER_STEPS - FFN_STEPS, 0)
-    row_of = lambda s: unit_of(s) // GROUPS
-    group_of = lambda s: unit_of(s) % GROUPS
-    by_row = lambda width: pl.BlockSpec((1, SEQ, width), lambda s: (layer_of(s), row_of(s), 0))
-    by_block = lambda width: pl.BlockSpec((1, BLOCK, width), lambda s: (layer_of(s), block_of(s), 0))
-    whole = lambda v: pl.BlockSpec(v.shape, lambda s: (0,) * v.ndim, pipeline_mode=pl.Buffered(1))
+    layer_of = lambda t: LAYERS - 1 - t
+    block_of = lambda p: jnp.minimum(p, FFN_STEPS - 1)
+    unit_of = lambda p: split(jnp.maximum(p - FFN_STEPS, 0))
+    row_of = lambda p: unit_of(p)[0]
+    by_row = lambda width: pl.BlockSpec((1, SEQ, width), lambda t, p: (layer_of(t), row_of(p), 0))
+    by_block = lambda width: pl.BlockSpec((1, BLOCK, width), lambda t, p: (layer_of(t), block_of(p), 0))
+    whole = lambda v: pl.BlockSpec(v.shape, lambda t, p: (0,) * v.ndim, pipeline_mode=pl.Buffered(1))
     shape = jax.ShapeDtypeStruct
     dma = pltpu.SemaphoreType.DMA
     return pl.pallas_call(
         backward_kernel,
-        grid=(LAYERS * LAYER_STEPS,),
+        grid=(LAYERS, LAYER_STEPS),
         in_specs=[
-            pl.BlockSpec((BLOCK, WIDTH), lambda s: (jnp.minimum(s, FFN_STEPS - 1), 0)),
-            pl.BlockSpec((1, BLOCK, WIDTH), lambda s: (layer_of(s) + 1, block_of(s), 0)),
+            pl.BlockSpec((BLOCK, WIDTH), lambda t, p: (jnp.where(t == 0, block_of(p), FFN_STEPS - 1), 0)),
+            pl.BlockSpec((1, BLOCK, WIDTH), lambda t, p: (layer_of(t) + 1, block_of(p), 0)),
             by_block(128), by_block(WIDTH), by_block(128), by_block(4 * CHUNK),
             by_row(WIDTH), by_row(2 * RANK), by_row(3 * WIDTH), by_row(WIDTH),
-            pl.BlockSpec((1, 1, GROUP, SEQ, SEQ), lambda s: (layer_of(s), row_of(s), group_of(s), 0, 0)),
-            pl.BlockSpec((1, 1, HEADS, 8, SEQ), lambda s: (layer_of(s), row_of(s), 0, 0, 0)),
+            pl.BlockSpec((1, 1, GROUP, SEQ, SEQ), lambda t, p: (layer_of(t), *unit_of(p), 0, 0)),
+            pl.BlockSpec((1, 1, HEADS, 8, SEQ), lambda t, p: (layer_of(t), row_of(p), 0, 0, 0)),
             whole(a), whole(b), whole(gains), anywhere, anywhere, anywhere,
         ],
         out_specs=[
-            pl.BlockSpec((SEQ, WIDTH), lambda s: (jnp.where(s < LAYER_STEPS * (LAYERS - 1), 0, row_of(s)), 0)),
-            pl.BlockSpec((LAYERS, 4 * RANK, WIDTH), lambda s: (0, 0, 0)),
+            pl.BlockSpec((SEQ, WIDTH), lambda t, p: (jnp.where(t < LAYERS - 1, 0, row_of(p)), 0)),
+            pl.BlockSpec((LAYERS, 4 * RANK, WIDTH), lambda t, p: (0, 0, 0)),
             anywhere,
         ],
         out_shape=[shape((TOKENS, WIDTH), F32), shape((LAYERS, 4 * RANK, WIDTH), F32), shape((TOKENS, WIDTH), BF)],
@@ -778,7 +835,7 @@
             pltpu.VMEM((4, 2, WIDTH, CHUNK), BF),
             dma((LAYERS, 2)), dma((4,)), dma,
         ],
-        compiler_params=params(1),
+        compiler_params=params(2),
         name="backward",
     )(cot, xall, r2, n1, r1, gd, xall, u, qkv, o, e, rinv, a, b, gains, wat, wf, xall)
 

time: 245 us -> 230 us (0.939)
  Pallas kernels: 238 us -> 223 us
    pallas_call x1, Pallas kernels: 133 us -> 122 us  [forward(): pl.pallas_call(functools.partial(forward_kernel, axes, direct), grid=(LAY...]
    pallas_call x1, Pallas kernels: 85.8 us -> 82.4 us  [backward(): pl.pallas_call(backward_kernel, grid=(LAYERS, LAYER_STEPS), in_specs=[pl....]
where the time goes in v1:
time: 230 us
  Pallas kernels  223 us (97%)
  local copies, waits for them, and re-layouts  5.06 us (2%)
    pallas_call x1, Pallas kernels, forward(): pl.pallas_call(functools.partial(forward_kernel, axes, direct), grid=(LAY...  122 us
    pallas_call x1, Pallas kernels, backward(): pl.pallas_call(backward_kernel, grid=(LAYERS, LAYER_STEPS), in_specs=[pl....  82.4 us
    pallas_call x1, Pallas kernels, all_sum(): pl.pallas_call(kernel, in_specs=[pl.BlockSpec(memory_space=pltpu.VMEM)],...  18.5 us

profile of v1, /device:TPU:0, one launch (start us, length us, event | category | flops | bytes accessed | tf_op | source)
XLA Modules:
  0.0 230.0 jit_solution(7251837616254107711)
XLA Ops:
  0.6 0.8 copy_add_fusion
  1.5 0.7 pad_maximum_fusion.b_ref
  2.1 0.8 slice_bitcast_fusion.5
  2.9 0.9 copy.28.a_ref
  3.8 121.8 %forward.1 = (bf16[2,1024,2304]{2,1,0:T(8,128)(2,1)}, bf16[2,1024,16]{2,1,0:T(8,128)(2,1)}, bf16[2,1024,768]{2,1,0:T(8,128)(2,1)}, bf16[2,2,12,512,512]{4,3,2,1,...) custom-call(s32[2]{0:T(128)} %len_ref.1, ...), custom_call_target="tpu_custom_call" | custom-call | tf_op jit(solution)/shard_map/forward/pallas_call | solution.py:617
  125.6 82.4 %backward.1 = (f32[1024,768]{1,0:T(8,128)}, f32[2,32,768]{2,1,0:T(8,128)}, bf16[1024,768]{1,0:T(8,128)(2,1)}) custom-call(bf16[1024,768]{1,0:T(8,128)(2,1)} %cot_ref.1, bf16[3,1024,768]{2,1,0:T(8,128)(2,1)} %get-tuple-element.19.x2_ref.x_ref.xall, f32[2,1024,128]{2,1,0:T(8,128)} %get-tuple-element.20.r2_ref, bf16[2,1024,768]{2,1,0:T(8,128)(2,1)} %get-tuple-element.21.n1_ref, ...), custom_call_target="tpu_custom_call" | custom-call | tf_op jit(solution)/shard_map/backward/pallas_call | solution.py:814
  208.1 1.7 reshape.20.v_ref
  209.8 18.5 %all_sum.1 = f32[32,12,128]{2,1,0:T(8,128)} custom-call(f32[32,12,128]{2,1,0:T(8,128)} %reshape.20.v_ref), custom_call_target="tpu_custom_call" | custom-call | tf_op jit(solution)/shard_map/all_sum/pallas_call | solution.py:364
  228.3 1.0 reshape.21
  229.3 0.7 slice_bitcast_fusion
  (3 shorter events, 0.0 us)

commit v2 on v1

--- a/solution.py
+++ b/solution.py
@@ -136,6 +136,9 @@
     elif what == "fown":
         for m, ref in enumerate((w1, w2)):
             remote(ref.at[layer], out.at[1, m], core_send.at[12 + m], core_recv.at[12 + m], place.to_core).start()
+    elif what == "fownin":
+        for m, ref in enumerate((w1, w2)):
+            remote(ref.at[layer], out.at[1, m], core_send.at[12 + m], core_recv.at[12 + m], place.to_core).wait()
     elif what == "fr" and tick < 4:
         s = 3 * g + tick - 1
         arrived(s)
@@ -169,8 +172,6 @@
     else:
         for s in range(12):
             remote(spot(1, s), spot(2, s), core_send.at[s], core_recv.at[s], place.to_core).wait()
-        for m, ref in enumerate((w1, w2)):
-            remote(ref.at[layer], out.at[1, m], core_send.at[12 + m], core_recv.at[12 + m], place.to_core).wait()
         for way in range(3):
             for i in range(4):
                 remote(spot(1, 0), spot(1, 0), send.at[way, i], recv.at[0], place.to_y).wait_send()
@@ -318,55 +319,108 @@
 
 
 def all_sum(axes, values, collective):
-    parts, high, wide = values.shape
-
-    def kernel(v_ref, out_ref, box, send, recv, send2, recv2):
+    layers, high, wide = values.shape
+    tiles = high // 8
+    owners = layers * tiles
+    chips = 4 * Z_SIZE
+    half = wide // 2
+
+    def kernel(v_ref, out_ref, sums, box, other_half, core_sem, send, recv, send2, recv2):
         place = Place(axes)
-        me = place.dp * 4 + place.t
+        core = place.core
+        me = place.dp * 2 + place.y
         barrier = pltpu.get_barrier_semaphore()
-
-        def peer(i):
-            other = lax.rem(me + i, parts)
-            return other, (other // 4, other % 4)
+        mine = pl.ds(pl.multiple_of(core * half, 128), half)
+        theirs = pl.ds(pl.multiple_of((1 - core) * half, 128), half)
+
+        def chip(i):
+            other = lax.rem(me + i, chips)
+            return other, (other // 2, (other % 2) * 2 + core)
+
+        def owner(k):
+            z, x = k // 2, k % 2
+            return k * 2 + (z + x) % 2, (k, (z + x) % 2 * 2 + core)
+
+        my_part = place.dp
+        is_owner = place.y == (place.z + place.x) % 2
+
+        def part(ref, k, columns):
+            return ref.at[k // tiles, pl.ds(pl.multiple_of(k % tiles * 8, 8), 8), columns]
 
         def signal(i, _):
-            pl.semaphore_signal(barrier, inc=1, device_id=peer(i)[1], device_id_type=MESH)
+            pl.semaphore_signal(barrier, inc=1, device_id=chip(i)[1], device_id_type=MESH)
             return 0
 
-        lax.fori_loop(1, parts, signal, 0)
-        pl.semaphore_wait(barrier, parts - 1)
-
-        def first(i, act):
-            other, device = peer(i)
-            act(remote(v_ref.at[other], box.at[i], send.at[i], recv.at[i], device))
+        pl.semaphore_signal(barrier, inc=1, device_id=place.to_core, device_id_type=MESH)
+        lax.fori_loop(1, chips, signal, 0)
+        pl.semaphore_wait(barrier, chips)
+        swap = remote(v_ref.at[:, :, theirs], other_half, core_sem.at[0], core_sem.at[1], place.to_core)
+        swap.start()
+        swap.wait()
+        sums[...] = v_ref[:, :, mine] + other_half[...]
+
+        def to_owner(k, act):
+            who, device = owner(k)
+
+            @pl.when(who != me)
+            def _():
+                act(remote(part(sums, k, slice(None)), box.at[me], send.at[k], recv.at[me], device))
+
             return 0
 
-        lax.fori_loop(1, parts, lambda i, _: first(i, lambda c: c.start()), 0)
-        lax.fori_loop(1, parts, lambda i, _: first(i, lambda c: c.wait()), 0)
-        out_ref[me] = v_ref[me] + jnp.sum(box[1:], axis=0)
-
-        def second(i, act):
-            other, device = peer(i)
-            act(remote(out_ref.at[me], out_ref.at[me], send2.at[i], recv2.at[i], device))
+        lax.fori_loop(0, owners, lambda k, _: to_owner(k, lambda c: c.start()), 0)
+
+        def collect(i, _):
+            other, device = chip(i)
+            remote(box.at[other], box.at[other], send.at[0], recv.at[other], device).wait_recv()
             return 0
 
-        lax.fori_loop(1, parts, lambda i, _: second(i, lambda c: c.start()), 0)
-
-        def finish(i, _):
-            other = lax.rem(me + parts - i, parts)
-            c = remote(out_ref.at[me], out_ref.at[other], send2.at[i], recv2.at[i], peer(i)[1])
-            c.wait()
+        def to_all(i, act):
+            other, device = chip(i)
+            spot = part(out_ref, my_part, mine)
+            act(remote(spot, spot, send2.at[i], recv2.at[my_part], device))
             return 0
 
-        lax.fori_loop(1, parts, finish, 0)
-
-    sem = pltpu.SemaphoreType.DMA((parts,))
+        @pl.when(is_owner)
+        def _():
+            lax.fori_loop(1, chips, collect, 0)
+            at = pl.ds(pl.multiple_of(my_part % tiles * 8, 8), 8)
+            box[me] = sums[my_part // tiles, at, :]
+            out_ref[my_part // tiles, at, mine] = jnp.sum(box[...], axis=0)
+            lax.fori_loop(1, chips, lambda i, _: to_all(i, lambda c: c.start()), 0)
+
+        def arrived(k, _):
+            who, device = owner(k)
+
+            @pl.when(who != me)
+            def _():
+                spot = part(out_ref, k, mine)
+                remote(spot, spot, send2.at[0], recv2.at[k], device).wait_recv()
+
+            return 0
+
+        lax.fori_loop(0, owners, arrived, 0)
+        swap = remote(out_ref.at[:, :, mine], out_ref.at[:, :, mine], core_sem.at[2], core_sem.at[3], place.to_core)
+        swap.start()
+        lax.fori_loop(0, owners, lambda k, _: to_owner(k, lambda c: c.wait_send()), 0)
+
+        @pl.when(is_owner)
+        def _():
+            lax.fori_loop(1, chips, lambda i, _: to_all(i, lambda c: c.wait_send()), 0)
+
+        swap.wait_send()
+        remote(out_ref.at[:, :, theirs], out_ref.at[:, :, theirs], core_sem.at[2], core_sem.at[3], place.to_core).wait_recv()
+
+    dma = pltpu.SemaphoreType.DMA
     return pl.pallas_call(
         kernel,
         in_specs=[pl.BlockSpec(memory_space=pltpu.VMEM)],
         out_specs=pl.BlockSpec(memory_space=pltpu.VMEM),
         out_shape=jax.ShapeDtypeStruct(values.shape, F32),
-        scratch_shapes=[pltpu.VMEM(values.shape, F32), sem, sem, sem, sem],
+        scratch_shapes=[
+            pltpu.VMEM((layers, high, half), F32), pltpu.VMEM((chips, 8, half), F32), pltpu.VMEM((layers, high, half), F32),
+            dma((4,)), dma((owners,)), dma((chips,)), dma((chips,)), dma((owners,)),
+        ],
         compiler_params=pltpu.CompilerParams(collective_id=collective, has_side_effects=True),
         name="all_sum",
     )(values)
@@ -380,7 +434,9 @@
 ATT_STEPS = ROWS * GROUPS
 FFN_STEPS = TOKENS // BLOCK
 LAYER_STEPS = ATT_STEPS + FFN_STEPS
-FORWARD_STEPS = ROWS + FFN_STEPS
+WIDE = 512
+WIDE_STEPS = TOKENS // WIDE
+FORWARD_STEPS = ROWS + 2 * WIDE_STEPS
 LAYERS = 2
 
 
@@ -438,31 +494,26 @@
     r1_ref[0] = jnp.broadcast_to(r, (SEQ, 128))
 
 
-def ffn_unit(block, w, gain, n1s, xs, gd_ref, r2_ref):
-    here = pl.ds(pl.multiple_of(block * BLOCK, BLOCK), BLOCK)
-    n1 = n1s[here, :]
-    f = n1.astype(F32)
-    for j in range(4):
+def ffn_unit(n1, f, chunks, w, gd_ref):
+    for i, j in enumerate(chunks):
         z = dot(n1, w[j, 0])
         cdf = 0.5 + 0.5 * lax.erf(z * 0.7071067811865476)
         pdf = jnp.exp2(z * (z * (-0.5 * 1.4426950408889634))) * 0.3989422804014327
-        gd_ref[0, :, CHUNK * j:CHUNK * (j + 1)] = (cdf + z * pdf).astype(BF)
+        gd_ref[0, :, CHUNK * i:CHUNK * (i + 1)] = (cdf + z * pdf).astype(BF)
         f = f + dot((z * cdf).astype(BF), w[j, 1])
-    m, r = norm_parts(f)
-    xs[here, :] = (m * gain).astype(BF)
-    r2_ref[0] = jnp.broadcast_to(r, (BLOCK, 128))
+    return f
 
 
 def forward_kernel(axes, direct, len_ref, tok, att, ex, pr, a_ref, b_ref, gain_ref,
                    qkv_ref, u_ref, o_ref, e_ref, rinv_ref, n1_ref, r1_ref, gd_ref, r2_ref, xall, wat_out, wf_out,
-                   xs, n1s, wat, wf, x_sem, xo_sem, wa_sem, wf_sem, own_sem, *sems):
+                   xs, n1s, fs, wat, wf, x_sem, xo_sem, wa_sem, wf_sem, own_sem, *sems):
     layer, part = pl.program_id(0), pl.program_id(1)
     step = layer * FORWARD_STEPS + part
     x_in = pltpu.make_async_copy(tok, xs, x_sem.at[0])
     x_out = pltpu.make_async_copy(xs, xall.at[0], x_sem.at[1])
 
     def save_x(l, b):
-        rows = pl.ds(pl.multiple_of(b * BLOCK, BLOCK), BLOCK)
+        rows = pl.ds(pl.multiple_of(b * WIDE, WIDE), WIDE)
         return pltpu.make_async_copy(xs.at[rows], xall.at[l + 1, rows], xo_sem.at[b])
 
     def save_attention(l):
@@ -484,7 +535,7 @@
 
         def run(job):
             what, l, *more = job
-            if what in ("fy", "fown", "fr", "ffin"):
+            if what in ("fy", "fown", "fownin", "fr", "ffin"):
                 ffn_gather(place, l, ex, pr, wf.at[l], ffn_sems[l], what, *more)
             else:
                 attention_gather(place, l, att, wat.at[l], att_sems[l], what, *more)
@@ -530,24 +581,33 @@
         attend_unit(part, len_ref[part], xs, wat.at[layer], a_ref.at[layer], b_ref.at[layer], gain_ref[layer, 0:1],
                     qkv_ref, u_ref, o_ref, e_ref, rinv_ref, n1_ref, r1_ref, n1s, lambda pair: slot(pair) if pair else None)
 
-    @pl.when(part >= ROWS)
-    def _():
-        block = part - ROWS
-
+    @pl.when((part >= ROWS) & (part < ROWS + WIDE_STEPS))
+    def _():
         @pl.when(step == ROWS)
         def _():
             x_out.wait()
 
+        here = pl.ds(pl.multiple_of((part - ROWS) * WIDE, WIDE), WIDE)
+        n1 = n1s[here, :]
+        fs[here, :] = ffn_unit(n1, n1.astype(F32), (0, 1), wf.at[layer], gd_ref)
+
+    @pl.when(part >= ROWS + WIDE_STEPS)
+    def _():
+        block = part - ROWS - WIDE_STEPS
+
         @pl.when(layer > 0)
         def _():
             save_x(layer - 1, block).wait()
 
-        ffn_unit(block, wf.at[layer], gain_ref[layer, 1:2], n1s, xs, gd_ref, r2_ref)
+        here = pl.ds(pl.multiple_of(block * WIDE, WIDE), WIDE)
+        m, r = norm_parts(ffn_unit(n1s[here, :], fs[here, :], (2, 3), wf.at[layer], gd_ref))
+        xs[here, :] = (m * gain_ref[layer, 1:2]).astype(BF)
+        r2_ref[0] = jnp.broadcast_to(r, (WIDE, 128))
         save_x(layer, block).start()
 
     @pl.when(step == LAYERS * FORWARD_STEPS - 1)
     def _():
-        for b in range(FFN_STEPS):
+        for b in range(WIDE_STEPS):
             save_x(LAYERS - 1, b).wait()
         if direct:
             for l in range(LAYERS):
@@ -557,49 +617,57 @@
 
 SCHEDULE = {
     (0, 0): [
-        ("line", 0, 0), ("fy", 0, 0), ("line", 0, 1), ("fr", 0, 1), ("fy", 0, 1), ("line", 0, 2),
-        ("side", 0, 0), ("side", 0, 1), ("side", 0, 2), ("fown", 0), ("line", 0, 3), ("line3", 0),
-        ("side", 0, 3), ("line", 1, 0), ("fy", 0, 2), ("fr", 0, 2), ("fy", 0, 3), ("far", 0, 0),
-        ("far", 0, 1), ("far", 0, 2), ("far", 0, 3), ("side3", 0), ("fin012", 0), ("line", 1, 1),
-        ("line", 1, 2),
+        ("line", 0, 0), ("fown", 1), ("fy", 0, 0), ("line", 0, 1), ("side", 0, 0), ("line", 0, 2),
+        ("fown", 0), ("side", 0, 1), ("line", 0, 3), ("far", 0, 0), ("line3", 0), ("side", 0, 2),
+        ("side", 0, 3), ("line", 1, 0), ("side3", 0), ("fy", 0, 1), ("far", 0, 1), ("fy", 0, 2), ("fy", 0, 3),
+        ("line", 1, 1), ("far", 0, 2), ("far", 0, 3), ("fin012", 0), ("fr", 0, 1),
     ],
     (0, 2): [
-        ("fr", 0, 3), ("side", 1, 0), ("far3", 0), ("line", 1, 3),
+        ("fownin", 0), ("far3", 0), ("fr", 0, 2),
     ],
     (0, 4): [
-        ("fin3", 0),
+        ("line", 1, 2), ("fy", 1, 0), ("fin3", 0),
     ],
     (1, 0): [
-        ("fr", 0, 4), ("fy", 1, 0), ("fr", 0, 5), ("fy", 1, 1), ("fown", 1),
+        ("fr", 0, 3),
     ],
     (1, 2): [
-        ("side", 1, 1), ("side", 1, 2), ("line3", 1), ("far", 1, 0),
+        ("side", 1, 0), ("fr", 0, 4),
     ],
     (1, 4): [
-        ("fr", 0, 6), ("fr", 1, 1), ("side", 1, 3),
+        ("line", 1, 3), ("side", 1, 1), ("fr", 0, 5),
     ],
     (2, 0): [
-        ("fr", 1, 2), ("ffin", 0),
+        ("fownin", 1), ("side", 1, 2),
     ],
     (3, 0): [
-        ("fy", 1, 2),
+        ("fr", 0, 6),
+    ],
+    (4, 0): [
+        ("side", 1, 3), ("line3", 1), ("ffin", 0),
     ],
     (5, 0): [
-        ("far", 1, 1), ("side3", 1), ("far", 1, 2), ("fy", 1, 3), ("far", 1, 3),
+        ("far", 1, 0), ("far", 1, 1), ("far", 1, 2), ("far", 1, 3), ("fy", 1, 1), ("fr", 1, 1),
     ],
     (6, 0): [
-        ("fr", 1, 3), ("fin012", 1),
+        ("side3", 1), ("fin012", 1), ("fy", 1, 2),
     ],
     (6, 2): [
-        ("far3", 1),
+        ("fy", 1, 3), ("fr", 1, 2), ("far3", 1),
     ],
     (6, 4): [
-        ("fin3", 1), ("fr", 1, 4), ("fr", 1, 5),
-    ],
-    (7, 2): [
+        ("fin3", 1),
+    ],
+    (7, 0): [
+        ("fr", 1, 3),
+    ],
+    (7, 4): [
+        ("fr", 1, 4), ("fr", 1, 5),
+    ],
+    (9, 0): [
         ("fr", 1, 6),
     ],
-    (8, 0): [
+    (10, 0): [
         ("ffin", 1),
     ],
 }
@@ -608,9 +676,12 @@
 def forward(axes, direct, lengths, tokens, att, ex, pr, a, b, gains):
     anywhere = pl.BlockSpec(memory_space=pl.ANY)
     row_of = lambda p: jnp.minimum(p, ROWS - 1)
-    block_of = lambda p: jnp.maximum(p - ROWS, 0)
     by_row = lambda width: pl.BlockSpec((1, SEQ, width), lambda l, p: (l, row_of(p), 0))
-    by_block = lambda width: pl.BlockSpec((1, BLOCK, width), lambda l, p: (l, block_of(p), 0))
+    def half_of(p):
+        i = jnp.maximum(p - ROWS, 0)
+        half = jnp.where(i >= WIDE_STEPS, 1, 0)
+        return i - half * WIDE_STEPS, half
+
     whole = lambda v: pl.BlockSpec(v.shape, lambda l, p: (0,) * v.ndim, pipeline_mode=pl.Buffered(1))
     shape = jax.ShapeDtypeStruct
     dma = pltpu.SemaphoreType.DMA
@@ -622,7 +693,10 @@
             by_row(3 * WIDTH), by_row(2 * RANK), by_row(WIDTH),
             pl.BlockSpec((1, 1, HEADS, SEQ, SEQ), lambda l, p: (l, row_of(p), 0, 0, 0)),
             pl.BlockSpec((1, 1, HEADS, 8, SEQ), lambda l, p: (l, row_of(p), 0, 0, 0)),
-            by_row(WIDTH), by_row(128), by_block(4 * CHUNK), by_block(128), anywhere, anywhere, anywhere,
+            by_row(WIDTH), by_row(128),
+            pl.BlockSpec((1, WIDE, 2 * CHUNK), lambda l, p: (l, *half_of(p))),
+            pl.BlockSpec((1, WIDE, 128), lambda l, p: (l, jnp.maximum(p - ROWS - WIDE_STEPS, 0), 0)),
+            anywhere, anywhere, anywhere,
         ],
         out_shape=[
             shape((LAYERS, TOKENS, 3 * WIDTH), BF), shape((LAYERS, TOKENS, 2 * RANK), BF), shape((LAYERS, TOKENS, WIDTH), BF),
@@ -633,9 +707,9 @@
             shape((LAYERS, 4 * WIDTH, WIDTH), BF), shape((LAYERS, 4, 2, WIDTH, CHUNK), BF),
         ],
         scratch_shapes=[
-            pltpu.VMEM((TOKENS, WIDTH), BF), pltpu.VMEM((TOKENS, WIDTH), BF),
+            pltpu.VMEM((TOKENS, WIDTH), BF), pltpu.VMEM((TOKENS, WIDTH), BF), pltpu.VMEM((TOKENS, WIDTH), F32),
             pltpu.VMEM((LAYERS, 4 * WIDTH, WIDTH), BF), pltpu.VMEM((LAYERS, 4, 2, WIDTH, CHUNK), BF),
-            dma((2,)), dma((FFN_STEPS,)), dma((LAYERS,)), dma((LAYERS,)), dma((LAYERS, 2)),
+            dma((2,)), dma((WIDE_STEPS,)), dma((LAYERS,)), dma((LAYERS,)), dma((LAYERS, 2)),
         ] + (ATT_SEMS * 2 + FFN_SEMS * 2 if direct else []),
         compiler_params=params(2, 0 if direct else None),
         name="forward",
@@ -857,7 +931,7 @@
         wat, wf = att, ex
     dx, grads, hidden = backward(cotangent, saved, a, b, gains, wat, wf)
     if direct:
-        total = all_sum(axes, grads.reshape(32, -1, 128), 1).reshape(grads.shape)
+        total = all_sum(axes, grads, 1)
     else:
         total = lax.psum(grads, axes)
     a_grad = total[:, :2 * RANK].reshape(LAYERS, 2, RANK, WIDTH).transpose(0, 1, 3, 2)

time: 230 us -> 221 us (0.961)
  Pallas kernels: 223 us -> 215 us
    pallas_call x1, Pallas kernels: 122 us -> 115 us  [forward(): pl.pallas_call(functools.partial(forward_kernel, axes, direct), grid=(LAY...]
    reshape x2 -> x0, local copies, waits for them, and re-layouts: 2.67 us -> none  [local(): total = all_sum(axes, grads.reshape(32, -1, 128), 1).reshape(grads.shape)]
where the time goes in v2:
time: 221 us; the launch traced here: 220 us
  Pallas kernels  215 us (97%)
  local copies, waits for them, and re-layouts  3.34 us (2%)
    pallas_call x1, Pallas kernels, forward(): pl.pallas_call(functools.partial(forward_kernel, axes, direct), grid=(LAY...  115 us
    pallas_call x1, Pallas kernels, backward(): pl.pallas_call(backward_kernel, grid=(LAYERS, LAYER_STEPS), in_specs=[pl....  82.3 us
    pallas_call x1, Pallas kernels, all_sum(): pl.pallas_call(kernel, in_specs=[pl.BlockSpec(memory_space=pltpu.VMEM)],...  17.9 us

profile of v2, /device:TPU:0, one launch (start us, length us, event | category | flops | bytes accessed | tf_op | source)
XLA Modules:
  0.0 220.4 jit_solution(5358567158631450500)
XLA Ops:
  0.6 0.8 copy_add_fusion
  1.5 0.7 pad_maximum_fusion.b_ref
  2.1 0.8 slice_bitcast_fusion.5
  2.9 0.9 copy.23.a_ref
  3.8 114.8 %forward.1 = (bf16[2,1024,2304]{2,1,0:T(8,128)(2,1)}, bf16[2,1024,16]{2,1,0:T(8,128)(2,1)}, bf16[2,1024,768]{2,1,0:T(8,128)(2,1)}, bf16[2,2,12,512,512]{4,3,2,1,...) custom-call(s32[2]{0:T(128)} %len_ref.1, ...), custom_call_target="tpu_custom_call" | custom-call | tf_op jit(solution)/shard_map/forward/pallas_call | solution.py:688
  118.6 82.3 %backward.1 = (f32[1024,768]{1,0:T(8,128)}, f32[2,32,768]{2,1,0:T(8,128)}, bf16[1024,768]{1,0:T(8,128)(2,1)}) custom-call(bf16[1024,768]{1,0:T(8,128)(2,1)} %cot_ref.1, bf16[3,1024,768]{2,1,0:T(8,128)(2,1)} %get-tuple-element.19.x2_ref.x_ref.xall, f32[2,1024,128]{2,1,0:T(8,128)} %get-tuple-element.20.r2_ref, bf16[2,1024,768]{2,1,0:T(8,128)(2,1)} %get-tuple-element.21.n1_ref, ...), custom_call_target="tpu_custom_call" | custom-call | tf_op jit(solution)/shard_map/backward/pallas_call | solution.py:888
  200.8 17.9 %all_sum.1 = f32[2,32,768]{2,1,0:T(8,128)} custom-call(f32[2,32,768]{2,1,0:T(8,128)} %get-tuple-element.33.v_ref), custom_call_target="tpu_custom_call" | custom-call | tf_op jit(solution)/shard_map/all_sum/pallas_call | solution.py:415
  218.8 1.6 slice_bitcast_fusion
  (3 shorter events, 0.0 us)

commit v3 on v2

--- a/solution.py
+++ b/solution.py
@@ -446,7 +446,7 @@
     return c * r, r
 
 
-def attend_unit(row, length, xs, w, a, b, gain, qkv_ref, u_ref, o_ref, e_ref, rinv_ref, n1_ref, r1_ref, n1s, slot):
+def attend_unit(row, length, xs, w, a, b, gain, qkv_ref, u_ref, o_ref, e_ref, rinv_ref, r1_ref, n1s, slot):
     here = pl.ds(pl.multiple_of(row * SEQ, SEQ), SEQ)
     x = xs[here, :]
     u = dot(x, a[...]).astype(BF)
@@ -455,7 +455,7 @@
         acc = dot(x, w[WIDTH * i:WIDTH * (i + 1), :])
         if i != 1:
             acc += dot(u, b[i // 2])
-        qkv_ref[0, :, WIDTH * i:WIDTH * (i + 1)] = acc.astype(BF)
+        qkv_ref[:, WIDTH * i:WIDTH * (i + 1)] = acc.astype(BF)
     key = lax.broadcasted_iota(jnp.int32, (SEQ, 128), 0)
     bound = jnp.where(key < length, 3.0e38, -8.0e9)
     lane = lax.broadcasted_iota(jnp.int32, (SEQ, 128), 1)
@@ -464,9 +464,9 @@
     for pair in range(HEADS // 2):
         slot(pair)
         at = pair * 128
-        q = qkv_ref[0, :, at:at + 128]
-        k = qkv_ref[0, :, WIDTH + at:WIDTH + at + 128]
-        v = qkv_ref[0, :, 2 * WIDTH + at:2 * WIDTH + at + 128]
+        q = qkv_ref[:, at:at + 128]
+        k = qkv_ref[:, WIDTH + at:WIDTH + at + 128]
+        v = qkv_ref[:, 2 * WIDTH + at:2 * WIDTH + at + 128]
         outs = []
         for half in range(2):
             mine = low if half == 0 else ~low
@@ -475,7 +475,7 @@
             s = jnp.minimum(dot_nt(k, qh), bound)
             top = jnp.max(s, axis=0, keepdims=True)
             e = jnp.exp2((s - top) * EXP2_SCALE).astype(BF)
-            e_ref[0, 0, pair * 2 + half] = e
+            e_ref[pair * 2 + half] = e
             ot = dot_tn(vh, e)
             if half == 0:
                 o_t, l = ot[:HEAD_DIM], ot[HEAD_DIM:HEAD_DIM + 8]
@@ -489,7 +489,6 @@
     slot(HEADS // 2)
     m, r = norm_parts(xs[here, :].astype(F32) + dot(o_ref[0], w[3 * WIDTH:, :]))
     n1 = (m * gain).astype(BF)
-    n1_ref[0] = n1
     n1s[here, :] = n1
     r1_ref[0] = jnp.broadcast_to(r, (SEQ, 128))
 
@@ -504,9 +503,15 @@
     return f
 
 
-def forward_kernel(axes, direct, len_ref, tok, att, ex, pr, a_ref, b_ref, gain_ref,
-                   qkv_ref, u_ref, o_ref, e_ref, rinv_ref, n1_ref, r1_ref, gd_ref, r2_ref, xall, wat_out, wf_out,
-                   xs, n1s, fs, wat, wf, x_sem, xo_sem, wa_sem, wf_sem, own_sem, *sems):
+def unit_columns(i):
+    row = lax.broadcasted_iota(jnp.int32, (RANK, 2 * RANK), 0)
+    column = lax.broadcasted_iota(jnp.int32, (RANK, 2 * RANK), 1)
+    return jnp.where(column == row + RANK * i, 1.0, 0.0).astype(BF)
+
+
+def forward_kernel(axes, direct, len_ref, tok, att, ex, pr, down_ref, up_ref, gain_ref,
+                   qkv_out, u_ref, o_ref, e_out, rinv_ref, n1_out, r1_ref, gd_ref, r2_ref, xall, wat_out, wf_out, a_out, b_out,
+                   qkv_s, e_s, a_ref, b_ref, xs, n1s, fs, wat, wf, row_sem, x_sem, xo_sem, wa_sem, wf_sem, own_sem, *sems):
     layer, part = pl.program_id(0), pl.program_id(1)
     step = layer * FORWARD_STEPS + part
     x_in = pltpu.make_async_copy(tok, xs, x_sem.at[0])
@@ -515,6 +520,15 @@
     def save_x(l, b):
         rows = pl.ds(pl.multiple_of(b * WIDE, WIDE), WIDE)
         return pltpu.make_async_copy(xs.at[rows], xall.at[l + 1, rows], xo_sem.at[b])
+
+    def save_row(l, row):
+        rows = pl.ds(pl.multiple_of(row * SEQ, SEQ), SEQ)
+        return (pltpu.make_async_copy(e_s.at[row], e_out.at[l, row], row_sem.at[0, row]),
+                pltpu.make_async_copy(qkv_s.at[row], qkv_out.at[l, rows], row_sem.at[1, row]),
+                pltpu.make_async_copy(n1s.at[rows], n1_out.at[l, rows], row_sem.at[3, row]))
+
+    save_adapters = (pltpu.make_async_copy(a_ref, a_out, row_sem.at[2, 0]),
+                     pltpu.make_async_copy(b_ref, b_out, row_sem.at[2, 1]))
 
     def save_attention(l):
         return pltpu.make_async_copy(wat.at[l], wat_out.at[l], wa_sem.at[l])
@@ -547,6 +561,14 @@
     @pl.when(step == 0)
     def _():
         x_in.start()
+        for l in range(LAYERS):
+            a_ref[l] = sum(dot_tn(down_ref[l, i], unit_columns(i)) for i in range(2)).astype(BF)
+            for i in range(2):
+                twice = up_ref[l, i].astype(F32) * 2.0
+                zero = jnp.zeros_like(twice)
+                b_ref[l, i] = jnp.concatenate([twice, zero] if i == 0 else [zero, twice], axis=0).astype(BF)
+        for c in save_adapters:
+            c.start()
         if direct:
             greet(place, True)
             for l in range(LAYERS):
@@ -578,8 +600,16 @@
 
     @pl.when(part < ROWS)
     def _():
+        @pl.when(layer > 0)
+        def _():
+            for c in save_row(layer - 1, part):
+                c.wait()
+
         attend_unit(part, len_ref[part], xs, wat.at[layer], a_ref.at[layer], b_ref.at[layer], gain_ref[layer, 0:1],
-                    qkv_ref, u_ref, o_ref, e_ref, rinv_ref, n1_ref, r1_ref, n1s, lambda pair: slot(pair) if pair else None)
+                    qkv_s.at[part], u_ref, o_ref, e_s.at[part], rinv_ref, r1_ref, n1s,
+                    lambda pair: slot(pair) if pair else None)
+        for c in save_row(layer, part):
+            c.start()
 
     @pl.when((part >= ROWS) & (part < ROWS + WIDE_STEPS))
     def _():
@@ -609,6 +639,11 @@
     def _():
         for b in range(WIDE_STEPS):
             save_x(LAYERS - 1, b).wait()
+        for c in save_adapters:
+            c.wait()
+        for row in range(ROWS):
+            for c in save_row(LAYERS - 1, row):
+                c.wait()
         if direct:
             for l in range(LAYERS):
                 save_attention(l).wait()
@@ -673,7 +708,7 @@
 }
 
 
-def forward(axes, direct, lengths, tokens, att, ex, pr, a, b, gains):
+def forward(axes, direct, lengths, tokens, att, ex, pr, down, up, gains):
     anywhere = pl.BlockSpec(memory_space=pl.ANY)
     row_of = lambda p: jnp.minimum(p, ROWS - 1)
     by_row = lambda width: pl.BlockSpec((1, SEQ, width), lambda l, p: (l, row_of(p), 0))
@@ -683,20 +718,20 @@
         return i - half * WIDE_STEPS, half
 
     whole = lambda v: pl.BlockSpec(v.shape, lambda l, p: (0,) * v.ndim, pipeline_mode=pl.Buffered(1))
+    a_shape, b_shape = (LAYERS, WIDTH, 2 * RANK), (LAYERS, 2, 2 * RANK, WIDTH)
     shape = jax.ShapeDtypeStruct
     dma = pltpu.SemaphoreType.DMA
     return pl.pallas_call(
         functools.partial(forward_kernel, axes, direct),
         grid=(LAYERS, FORWARD_STEPS),
-        in_specs=[pl.BlockSpec(memory_space=pltpu.SMEM)] + [anywhere] * 4 + [whole(a), whole(b), whole(gains)],
+        in_specs=[pl.BlockSpec(memory_space=pltpu.SMEM)] + [anywhere] * 4 + [whole(down), whole(up), whole(gains)],
         out_specs=[
-            by_row(3 * WIDTH), by_row(2 * RANK), by_row(WIDTH),
-            pl.BlockSpec((1, 1, HEADS, SEQ, SEQ), lambda l, p: (l, row_of(p), 0, 0, 0)),
+            anywhere, by_row(2 * RANK), by_row(WIDTH), anywhere,
             pl.BlockSpec((1, 1, HEADS, 8, SEQ), lambda l, p: (l, row_of(p), 0, 0, 0)),
-            by_row(WIDTH), by_row(128),
+            anywhere, by_row(128),
             pl.BlockSpec((1, WIDE, 2 * CHUNK), lambda l, p: (l, *half_of(p))),
             pl.BlockSpec((1, WIDE, 128), lambda l, p: (l, jnp.maximum(p - ROWS - WIDE_STEPS, 0), 0)),
-            anywhere, anywhere, anywhere,
+            anywhere, anywhere, anywhere, anywhere, anywhere,
         ],
         out_shape=[
             shape((LAYERS, TOKENS, 3 * WIDTH), BF), shape((LAYERS, TOKENS, 2 * RANK), BF), shape((LAYERS, TOKENS, WIDTH), BF),
@@ -704,16 +739,18 @@
             shape((LAYERS, TOKENS, WIDTH), BF), shape((LAYERS, TOKENS, 128), F32),
             shape((LAYERS, TOKENS, 4 * CHUNK), BF), shape((LAYERS, TOKENS, 128), F32),
             shape((LAYERS + 1, TOKENS, WIDTH), BF),
-            shape((LAYERS, 4 * WIDTH, WIDTH), BF), shape((LAYERS, 4, 2, WIDTH, CHUNK), BF),
+            shape((LAYERS, 4 * WIDTH, WIDTH), BF), shape((LAYERS, 4, 2, WIDTH, CHUNK), BF), shape(a_shape, BF), shape(b_shape, BF),
         ],
         scratch_shapes=[
+            pltpu.VMEM((ROWS, SEQ, 3 * WIDTH), BF), pltpu.VMEM((ROWS, HEADS, SEQ, SEQ), BF),
+            pltpu.VMEM(a_shape, BF), pltpu.VMEM(b_shape, BF),
             pltpu.VMEM((TOKENS, WIDTH), BF), pltpu.VMEM((TOKENS, WIDTH), BF), pltpu.VMEM((TOKENS, WIDTH), F32),
             pltpu.VMEM((LAYERS, 4 * WIDTH, WIDTH), BF), pltpu.VMEM((LAYERS, 4, 2, WIDTH, CHUNK), BF),
-            dma((2,)), dma((WIDE_STEPS,)), dma((LAYERS,)), dma((LAYERS,)), dma((LAYERS, 2)),
+            dma((4, ROWS)), dma((2,)), dma((WIDE_STEPS,)), dma((LAYERS,)), dma((LAYERS,)), dma((LAYERS, 2)),
         ] + (ATT_SEMS * 2 + FFN_SEMS * 2 if direct else []),
         compiler_params=params(2, 0 if direct else None),
         name="forward",
-    )(lengths, tokens, att, ex, pr, a, b, gains)
+    )(lengths, tokens, att, ex, pr, down, up, gains)
 
 
 def norm_back(e, m, r):
@@ -915,10 +952,6 @@
 
 
 def local(axes, direct, tokens, lengths, attention, down, up, expand, project, gains, cotangent):
-    a = jnp.concatenate([down[:, 0], down[:, 1]], axis=2)
-    twice = up + up
-    b = jnp.stack([jnp.pad(twice[:, 0], ((0, 0), (0, RANK), (0, 0))), jnp.pad(twice[:, 1], ((0, 0), (RANK, 0), (0, 0)))],
-                  axis=1)
     if direct:
         att, ex, pr = attention, expand, project
     else:
@@ -926,7 +959,7 @@
         w1 = lax.all_gather(expand, axes[1], axis=2, tiled=True).reshape(LAYERS, WIDTH, 4, CHUNK).transpose(0, 2, 1, 3)
         w2 = lax.all_gather(project, axes[1], axis=1, tiled=True).reshape(LAYERS, 4, CHUNK, WIDTH)
         ex = pr = jnp.stack([w1, w2], axis=2)
-    *saved, wat, wf = forward(axes, direct, lengths, tokens, att, ex, pr, a, b, gains)
+    *saved, wat, wf, a, b = forward(axes, direct, lengths, tokens, att, ex, pr, down.swapaxes(2, 3), up, gains)
     if not direct:
         wat, wf = att, ex
     dx, grads, hidden = backward(cotangent, saved, a, b, gains, wat, wf)

time: 221 us -> 215 us (0.973)
  Pallas kernels: 215 us -> 212 us
    pallas_call x1, Pallas kernels: 115 us -> 112 us  [forward(): pl.pallas_call(functools.partial(forward_kernel, axes, direct), grid=(LAY...]
where the time goes in v3:
time: 215 us; the launch traced here: 214 us
  Pallas kernels  212 us (99%)
    pallas_call x1, Pallas kernels, forward(): pl.pallas_call(functools.partial(forward_kernel, axes, direct), grid=(LAY...  112 us
    pallas_call x1, Pallas kernels, backward(): pl.pallas_call(backward_kernel, grid=(LAYERS, LAYER_STEPS), in_specs=[pl....  82.3 us
    pallas_call x1, Pallas kernels, all_sum(): pl.pallas_call(kernel, in_specs=[pl.BlockSpec(memory_space=pltpu.VMEM)],...  17.9 us

profile of v3, /device:TPU:0, one launch (start us, length us, event | category | flops | bytes accessed | tf_op | source)
XLA Modules:
  0.0 214.4 jit_solution(12195535912348757589)
XLA Ops:
  0.6 111.9 %forward.1 = (bf16[2,1024,2304]{2,1,0:T(8,128)(2,1)}, bf16[2,1024,16]{2,1,0:T(8,128)(2,1)}, bf16[2,1024,768]{2,1,0:T(8,128)(2,1)}, bf16[2,2,12,512,512]{4,3,2,1,...) custom-call(s32[2]{0:T(128)} %len_ref.1, ...), custom_call_target="tpu_custom_call" | custom-call | tf_op jit(solution)/shard_map/forward/pallas_call | solution.py:724
  112.6 82.3 %backward.1 = (f32[1024,768]{1,0:T(8,128)}, f32[2,32,768]{2,1,0:T(8,128)}, bf16[1024,768]{1,0:T(8,128)(2,1)}) custom-call(bf16[1024,768]{1,0:T(8,128)(2,1)} %cot_ref.1, bf16[3,1024,768]{2,1,0:T(8,128)(2,1)} %get-tuple-element.21.x2_ref.x_ref.xall, f32[2,1024,128]{2,1,0:T(8,128)} %get-tuple-element.22.r2_ref, bf16[2,1024,768]{2,1,0:T(8,128)(2,1)} %get-tuple-element.23.n1_ref, ...), custom_call_target="tpu_custom_call" | custom-call | tf_op jit(solution)/shard_map/backward/pallas_call | solution.py:925
  194.8 17.9 %all_sum.1 = f32[2,32,768]{2,1,0:T(8,128)} custom-call(f32[2,32,768]{2,1,0:T(8,128)} %get-tuple-element.37.v_ref), custom_call_target="tpu_custom_call" | custom-call | tf_op jit(solution)/shard_map/all_sum/pallas_call | solution.py:415
  212.8 1.6 slice_bitcast_fusion

commit v4 on v3

--- a/solution.py
+++ b/solution.py
@@ -325,6 +325,10 @@
     chips = 4 * Z_SIZE
     half = wide // 2
 
+    def each(start, stop, body, carry):
+        for i in range(start, stop):
+            body(i, carry)
+
     def kernel(v_ref, out_ref, sums, box, other_half, core_sem, send, recv, send2, recv2):
         place = Place(axes)
         core = place.core
@@ -352,7 +356,7 @@
             return 0
 
         pl.semaphore_signal(barrier, inc=1, device_id=place.to_core, device_id_type=MESH)
-        lax.fori_loop(1, chips, signal, 0)
+        each(1, chips, signal, 0)
         pl.semaphore_wait(barrier, chips)
         swap = remote(v_ref.at[:, :, theirs], other_half, core_sem.at[0], core_sem.at[1], place.to_core)
         swap.start()
@@ -368,7 +372,7 @@
 
             return 0
 
-        lax.fori_loop(0, owners, lambda k, _: to_owner(k, lambda c: c.start()), 0)
+        each(0, owners, lambda k, _: to_owner(k, lambda c: c.start()), 0)
 
         def collect(i, _):
             other, device = chip(i)
@@ -383,11 +387,11 @@
 
         @pl.when(is_owner)
         def _():
-            lax.fori_loop(1, chips, collect, 0)
+            each(1, chips, collect, 0)
             at = pl.ds(pl.multiple_of(my_part % tiles * 8, 8), 8)
             box[me] = sums[my_part // tiles, at, :]
             out_ref[my_part // tiles, at, mine] = jnp.sum(box[...], axis=0)
-            lax.fori_loop(1, chips, lambda i, _: to_all(i, lambda c: c.start()), 0)
+            each(1, chips, lambda i, _: to_all(i, lambda c: c.start()), 0)
 
         def arrived(k, _):
             who, device = owner(k)
@@ -399,14 +403,14 @@
 
             return 0
 
-        lax.fori_loop(0, owners, arrived, 0)
+        each(0, owners, arrived, 0)
         swap = remote(out_ref.at[:, :, mine], out_ref.at[:, :, mine], core_sem.at[2], core_sem.at[3], place.to_core)
         swap.start()
-        lax.fori_loop(0, owners, lambda k, _: to_owner(k, lambda c: c.wait_send()), 0)
+        each(0, owners, lambda k, _: to_owner(k, lambda c: c.wait_send()), 0)
 
         @pl.when(is_owner)
         def _():
-            lax.fori_loop(1, chips, lambda i, _: to_all(i, lambda c: c.wait_send()), 0)
+            each(1, chips, lambda i, _: to_all(i, lambda c: c.wait_send()), 0)
 
         swap.wait_send()
         remote(out_ref.at[:, :, theirs], out_ref.at[:, :, theirs], core_sem.at[2], core_sem.at[3], place.to_core).wait_recv()

time: 215 us -> 215 us (level)
  no operation moved by 1% of the time
where the time goes in v4:
time: 215 us; the launch traced here: 214 us
  Pallas kernels  212 us (99%)
    pallas_call x1, Pallas kernels, forward(): pl.pallas_call(functools.partial(forward_kernel, axes, direct), grid=(LAY...  112 us
    pallas_call x1, Pallas kernels, backward(): pl.pallas_call(backward_kernel, grid=(LAYERS, LAYER_STEPS), in_specs=[pl....  82.3 us
    pallas_call x1, Pallas kernels, all_sum(): pl.pallas_call(kernel, in_specs=[pl.BlockSpec(memory_space=pltpu.VMEM)],...  17.8 us

profile of v4, /device:TPU:0, one launch (start us, length us, event | category | flops | bytes accessed | tf_op | source)
XLA Modules:
  0.0 214.3 jit_solution(2179916955663150345)
XLA Ops:
  0.6 111.9 %forward.1 = (bf16[2,1024,2304]{2,1,0:T(8,128)(2,1)}, bf16[2,1024,16]{2,1,0:T(8,128)(2,1)}, bf16[2,1024,768]{2,1,0:T(8,128)(2,1)}, bf16[2,2,12,512,512]{4,3,2,1,...) custom-call(s32[2]{0:T(128)} %len_ref.1, ...), custom_call_target="tpu_custom_call" | custom-call | tf_op jit(solution)/shard_map/forward/pallas_call | solution.py:728
  112.6 82.3 %backward.1 = (f32[1024,768]{1,0:T(8,128)}, f32[2,32,768]{2,1,0:T(8,128)}, bf16[1024,768]{1,0:T(8,128)(2,1)}) custom-call(bf16[1024,768]{1,0:T(8,128)(2,1)} %cot_ref.1, bf16[3,1024,768]{2,1,0:T(8,128)(2,1)} %get-tuple-element.21.x2_ref.x_ref.xall, f32[2,1024,128]{2,1,0:T(8,128)} %get-tuple-element.22.r2_ref, bf16[2,1024,768]{2,1,0:T(8,128)(2,1)} %get-tuple-element.23.n1_ref, ...), custom_call_target="tpu_custom_call" | custom-call | tf_op jit(solution)/shard_map/backward/pallas_call | solution.py:929
  194.8 17.8 %all_sum.1 = f32[2,32,768]{2,1,0:T(8,128)} custom-call(f32[2,32,768]{2,1,0:T(8,128)} %get-tuple-element.37.v_ref), custom_call_target="tpu_custom_call" | custom-call | tf_op jit(solution)/shard_map/all_sum/pallas_call | solution.py:419
  212.7 1.6 slice_bitcast_fusion
